TPU v7x, 256 devices: a whole 4x4x8 slice. The times are simulated.
256 devices in a mesh: grp: 4 (over x), dom: 64 (over y, z, core).
Axes of the slice: x: 4, y: 4, z: 8, core: 2. Of those that a mesh axis runs over, the one named last changes fastest.
Arguments:
- state: float32 [65536, 12, 128], P(('grp', 'dom'))
- neighbours: int32 [65536, 4], P(('grp', 'dom')), may hold values from 0 to 511
- pair_mask: int32 [65536, 4], P(('grp', 'dom')), may hold values from 0 to 1, as said below
- send_lists: int32 [256, 4, 64], P(('grp', 'dom')), may hold values from 0 to 255, as said below
- send_counts: int32 [256, 4], P(('grp', 'dom')), may hold values from 1 to 64, as said below
- movers: int32 [256, 64, 16], P(('grp', 'dom')), may hold values from 0 to 32767, as said below
- mover_counts: int32 [256, 64], P(('grp', 'dom')), may hold values from 0 to 16, as said below
Outputs:
- kept: float32 [65536, 12, 128], P(('grp', 'dom'))
- arrivals: float32 [12, 262144], P(None, ('grp', 'dom'))
Inputs may be any that keep to these rules, and one draw needn't show every extreme that they name: `neighbours`: below 256: the device's own blocks; then 64 slots from each of lower domain, upper domain, lower slab, upper slab. `pair_mask`: 1 marks a live pair block, 0 padding. `send_lists`: each list holds distinct own block numbers. `send_counts`: on each device one of the four lists is full. `movers`: all particle numbers of a device are distinct. `mover_counts`: zero toward the device's own domain; on each device some other domain gets 16.
All inputs are finite; a program needn't handle non-finite values.
Results may differ from a plain program's by a relative error of at most 0.00007.
Values sent between devices are 32-bit elements; how exact they have to be, the bound alone decides.
A program may use at most 64 MiB of HBM per device.

v0:
```python
import jax
import jax.numpy as jnp
from jax import lax
from jax.sharding import PartitionSpec as P


def with_halo(shard, sides, width):
    for axis, dim in sides:
        size, length = (lax.axis_size(axis), shard.shape[dim])
        up = [(i, (i + 1) % size) for i in range(size - 1)]
        down = [(j, i) for i, j in up]
        last = lax.slice_in_dim(shard, length - width, length, axis=dim)
        initial = lax.slice_in_dim(shard, 0, width, axis=dim)
        before = lax.ppermute(last, axis, up)
        after = lax.ppermute(initial, axis, down)
        shard = jnp.concatenate([before, shard, after], axis=dim)
    return shard


def payload(state):
    mass = state[:, 6]
    volume = mass / state[:, 7]
    return jnp.concatenate(
        [state[:, 0:3], mass[:, None], volume[:, None], state[:, 8:11], state[:, 3:6]], axis=1
    )


def kernel_weights(own_pos, near_pos, alive_flags):
    radius = None
    for comp in range(3):
        delta = own_pos[..., comp, :, None] - near_pos[..., comp, None, :]
        radius = delta * delta if radius is None else radius + delta * delta
    smoothing_kernel = jnp.maximum(0.0, 1.0 - 2.0 * radius)
    return smoothing_kernel * smoothing_kernel * smoothing_kernel * alive_flags[..., None, None]


def advance(state, sums):
    position = state[:, 0:3]
    velocity = state[:, 3:6]
    temper = state[:, 8]
    solute_one = state[:, 9]
    solute_two = state[:, 10]
    solid = state[:, 11]
    sum_volume = sums[:, 1]
    temp_one = temper + 0.25 * (sums[:, 2] - temper * sum_volume)
    conc_one = solute_one + 0.2 * (sums[:, 3] - solute_one * sum_volume)
    conc_two = solute_two + 0.1 * (sums[:, 4] - solute_two * sum_volume)
    velocity_new = velocity + 0.3 * (sums[:, 5:8] - velocity * sum_volume[:, None])
    position_new = position + 0.02 * velocity_new
    liquidus = 1.0 - 0.3 * conc_one - 0.2 * conc_two
    solid_new = jnp.maximum(solid, jnp.clip(2.0 * (liquidus - temp_one), 0.0, 1.0))
    temp_two = temp_one + 0.4 * (solid_new - solid)
    solute_first_updated = conc_one * (1.0 - 0.83 * solid) / (1.0 - 0.83 * solid_new)
    conc_two_new = conc_two * (1.0 - 0.6 * solid) / (1.0 - 0.6 * solid_new)
    return jnp.concatenate(
        [
            position_new,
            velocity_new,
            state[:, 6:7],
            sums[:, 0:1],
            temp_two[:, None],
            solute_first_updated[:, None],
            conc_two_new[:, None],
            solid_new[:, None],
        ],
        axis=1,
    )


def on_device(state, neighbours, pair_mask, send_lists, send_counts, movers, mover_counts):
    blocks = state.shape[0]
    width = neighbours.shape[1]
    slots = send_lists.shape[2]
    own = payload(state)
    outgoing = own[send_lists[0]]
    filled = (jnp.arange(slots, dtype=jnp.int32)[None, :] < send_counts[0][:, None]).astype(
        jnp.float32
    )
    outgoing = outgoing * filled[:, :, None, None]
    along_dom = with_halo(jnp.stack([outgoing[0], outgoing[1]]), (("dom", 0),), 1)
    along_grp = with_halo(jnp.stack([outgoing[2], outgoing[3]]), (("grp", 0),), 1)
    from_lower = along_grp[0]
    from_upper = along_grp[3]
    candidates = jnp.concatenate([own, along_dom[0], along_dom[3], from_lower, from_upper], axis=0)
    volume = candidates[:, 4]
    carried = jnp.concatenate([candidates[:, 3:5], volume[:, None] * candidates[:, 5:11]], axis=1)
    table = jnp.concatenate(
        [candidates[:, 0:3], jnp.zeros((candidates.shape[0], 5, 128), jnp.float32), carried], axis=1
    )
    own_pos = state[:, 0:3]
    group = min(16, blocks)
    live_all = pair_mask.astype(jnp.float32)

    def one_group(items):
        pos_group, nbr_group, live_group = items
        nearby_particles = table[nbr_group]
        kernel_weight = kernel_weights(pos_group[:, None], nearby_particles[:, :, 0:3], live_group)
        return jnp.einsum(
            "gkij,gkcj->gci",
            kernel_weight,
            nearby_particles[:, :, 8:16],
            precision=lax.Precision.HIGHEST,
        )

    sums = lax.map(
        one_group,
        (
            own_pos.reshape(blocks // group, group, 3, 128),
            neighbours.reshape(blocks // group, group, width),
            live_all.reshape(blocks // group, group, width),
        ),
    )
    sums = sums.reshape(blocks, 8, 128)
    updated = advance(state, sums)
    picked = movers[0].reshape(-1)
    per_dest = movers.shape[2]
    sending = (
        (jnp.arange(per_dest, dtype=jnp.int32)[None, :] < mover_counts[0][:, None])
        .astype(jnp.float32)
        .reshape(-1)
    )
    block_of = picked // 128
    lane_of = picked % 128
    leaving = updated[block_of, :, lane_of] * sending[:, None]
    outbound = leaving.T
    arrivals = lax.all_to_all(outbound, "dom", split_axis=1, concat_axis=1, tiled=True)
    departed = jnp.zeros((blocks, 128), jnp.float32).at[block_of, lane_of].max(sending)
    kept = updated * (1.0 - departed)[:, None, :]
    return (kept, arrivals)


def solution(mesh):
    placed = (
        P(("grp", "dom"), None, None),
        P(("grp", "dom"), None),
        P(("grp", "dom"), None),
        P(("grp", "dom"), None, None),
        P(("grp", "dom"), None),
        P(("grp", "dom"), None, None),
        P(("grp", "dom"), None),
    )
    return jax.shard_map(
        on_device,
        mesh=mesh,
        in_specs=placed,
        out_specs=(P(("grp", "dom"), None, None), P(None, ("grp", "dom"))),
        check_vma=False,
    )
```

profile of v0, /device:TPU:1, one launch (start us, length us, event | category | flops | bytes accessed | tf_op | source)
XLA Modules:
  0.0 253.1 jit_solution(13311066718599511244)
XLA Ops:
  0.6 2.0 fusion.44
  7.4 2.2 copy.117
  9.8 3.7 %gather_fusion.1 = f32[256,11,128]{2,1,0:T(8,128)} fusion(f32[256,11,128]{2,1,0:T(8,128)} %copy.117, s32[1024]{0:T(1024)S(1)} %pad_clamp_fusion.1), kind=kCustom, calls=%fused_computation.1 | custom fusion | bytes 2884608 | tf_op jit(solution)/shard_map/gather | solution.py:75
  13.5 2.1 copy.118
  17.1 4.9 %collective-permute-start = (f32[1,64,11,128]{3,1,2,0:T(8,128)}, f32[1,64,11,128]{3,1,2,0:T(8,128)}, u32[]{:S(2)}, u32[]{:S(2)}) collective-permute-start(f32[1,64,11,128]{3,1,2,0:T(8,128)} %get-tuple-element.98), channel_id=1, source_target_pairs={{0,1},{1,2},{2,3},{3,4},{4,5},{5,6},{6,7},{7,8},{8,9},{9,10},{10,1... | collective-permute-start | bytes 1081352 | tf_op jit(solution)/shard_map/ppermute | solution.py:14
  22.1 2.2 collective-permute-start.1
  24.3 2.8 %collective-permute-start.2 = (f32[1,64,11,128]{3,1,2,0:T(8,128)}, f32[1,64,11,128]{3,1,2,0:T(8,128)S(1)}, u32[]{:S(2)}, u32[]{:S(2)}) collective-permute-start(f32[1,64,11,128]{3,1,2,0:T(8,128)} %get-tuple-element.96), channel_id=1, source_target_pairs={{0,64},{64,128},{128,192},{1,65},{65,129},{129,193},{2,66},{66,130... | collective-permute-start | bytes 1081352 | tf_op jit(solution)/shard_map/ppermute | solution.py:14
  29.3 6.0 %scatter_custom_fusion = f32[32768]{0:T(1024)S(1)} fusion(s32[1024]{0:T(1024)S(1)} %broadcast_select_fusion, f32[1024]{0:T(1024)S(1)} %reshape.282, f32[]{:T(128)} %constant.33.clone.1), kind=kCustom, calls=%fused_computation.84 | custom fusion | flops 1024 | bytes 131076
  35.3 1.8 bitcast_dynamic-update-slice_fusion.3
  37.1 1.8 bitcast_dynamic-update-slice_fusion.2
  47.1 2.6 %pad_maximum_fusion = f32[512,16,128]{2,1,0:T(8,128)} fusion(f32[512,6,128]{2,1,0:T(8,128)S(1)} %copy.125, f32[512,2,128]{2,1,0:T(2,128)S(1)} %copy.124, f32[512,3,128]{2,1,0:T(4,128)S(1)} %copy.123, f32[16]{0:T(128)S(1)} %pad.3.clone), kind=kLoop, calls=%fused_computation.42 | loop fusion | flops 3145728 | bytes 7077952 | tf_op jit(solution)/shard_map/concatenate | solution.py:87
  49.7 154.3 %while.10 = (s32[]{:T(128)}, f32[16,16,8,128]{3,1,0,2:T(8,128)}, s32[16,16,4]{1,0,2:T(8,128)S(1)}, f32[512,16,128]{2,1,0:T(8,128)}, f32[16,16,3,128]{3,1,0,2:T(8,128)S(1)}, /*index=5*/f32[16,16,4]{1,0,2:T(8,128)S(1)}, s32[]{:T(128)}) while((s32[]{:T(128)}, f32[16,16,8,128]{3,1,0,2:T(8,128)}, s32[16,16,4]{1,0,2:T(8,128)S(1)}, ...), condition=%wide.region_1.2_spmd, body=%wide.region_0.1_spmd.sunk | while | flops 115344576 | bytes 1941593 | solution.py:105
  49.9 2.8 %gather_fusion = f32[64,16,128]{2,1,0:T(8,128)S(1)} fusion(f32[512,16,128]{2,1,0:T(8,128)} %get-tuple-element.165, s32[1024]{0:T(1024)S(1)} %pad_clamp_fusion.3), kind=kCustom, calls=%fused_computation.clone.1 | custom fusion | bytes 1048832 | tf_op jit(solution)/shard_map/while/body/eval_jaxpr/gather | solution.py:96
  52.9 5.8 %fusion.52 = f32[1,16,8,128]{3,2,1,0:T(8,128)S(1)} fusion(f32[16,4]{1,0:T(8,128)S(1)} %copy.145, f32[16,4,128]{2,1,0:T(4,128)S(1)} %bitcast.101, f32[16,128]{1,0:T(8,128)S(1)} %get-tuple-element.143, f32[16,4,128]{2,1,0:T(4,128)S(1)} %bitcast.100, f32[16,128]{1,0:T(8,128)S(1)} %get-tuple-element.145, f32[16,4,128]{2,1,0:T(4,128)S(1)} %bitcast.99, ...), kind=kOutput, calls=%fused_computation.28.clone.1 | convolution fusion | flops 115343360 | bytes 458752 | tf_op jit(solution)/shard_map/while/body/eval_jaxpr/gkij,gkcj->gci/dot_general | solution.py:98
  59.6 2.8 %gather_fusion = f32[64,16,128]{2,1,0:T(8,128)S(1)} fusion(f32[512,16,128]{2,1,0:T(8,128)} %get-tuple-element.165, s32[1024]{0:T(1024)S(1)} %pad_clamp_fusion.3), kind=kCustom, calls=%fused_computation.clone.1 | custom fusion | bytes 1048832 | tf_op jit(solution)/shard_map/while/body/eval_jaxpr/gather | solution.py:96
  62.6 5.8 %fusion.52 = f32[1,16,8,128]{3,2,1,0:T(8,128)S(1)} fusion(f32[16,4]{1,0:T(8,128)S(1)} %copy.145, f32[16,4,128]{2,1,0:T(4,128)S(1)} %bitcast.101, f32[16,128]{1,0:T(8,128)S(1)} %get-tuple-element.143, f32[16,4,128]{2,1,0:T(4,128)S(1)} %bitcast.100, f32[16,128]{1,0:T(8,128)S(1)} %get-tuple-element.145, f32[16,4,128]{2,1,0:T(4,128)S(1)} %bitcast.99, ...), kind=kOutput, calls=%fused_computation.28.clone.1 | convolution fusion | flops 115343360 | bytes 458752 | tf_op jit(solution)/shard_map/while/body/eval_jaxpr/gkij,gkcj->gci/dot_general | solution.py:98
  69.2 2.8 %gather_fusion = f32[64,16,128]{2,1,0:T(8,128)S(1)} fusion(f32[512,16,128]{2,1,0:T(8,128)} %get-tuple-element.165, s32[1024]{0:T(1024)S(1)} %pad_clamp_fusion.3), kind=kCustom, calls=%fused_computation.clone.1 | custom fusion | bytes 1048832 | tf_op jit(solution)/shard_map/while/body/eval_jaxpr/gather | solution.py:96
  72.2 5.8 %fusion.52 = f32[1,16,8,128]{3,2,1,0:T(8,128)S(1)} fusion(f32[16,4]{1,0:T(8,128)S(1)} %copy.145, f32[16,4,128]{2,1,0:T(4,128)S(1)} %bitcast.101, f32[16,128]{1,0:T(8,128)S(1)} %get-tuple-element.143, f32[16,4,128]{2,1,0:T(4,128)S(1)} %bitcast.100, f32[16,128]{1,0:T(8,128)S(1)} %get-tuple-element.145, f32[16,4,128]{2,1,0:T(4,128)S(1)} %bitcast.99, ...), kind=kOutput, calls=%fused_computation.28.clone.1 | convolution fusion | flops 115343360 | bytes 458752 | tf_op jit(solution)/shard_map/while/body/eval_jaxpr/gkij,gkcj->gci/dot_general | solution.py:98
  78.9 2.8 %gather_fusion = f32[64,16,128]{2,1,0:T(8,128)S(1)} fusion(f32[512,16,128]{2,1,0:T(8,128)} %get-tuple-element.165, s32[1024]{0:T(1024)S(1)} %pad_clamp_fusion.3), kind=kCustom, calls=%fused_computation.clone.1 | custom fusion | bytes 1048832 | tf_op jit(solution)/shard_map/while/body/eval_jaxpr/gather | solution.py:96
  81.9 5.8 %fusion.52 = f32[1,16,8,128]{3,2,1,0:T(8,128)S(1)} fusion(f32[16,4]{1,0:T(8,128)S(1)} %copy.145, f32[16,4,128]{2,1,0:T(4,128)S(1)} %bitcast.101, f32[16,128]{1,0:T(8,128)S(1)} %get-tuple-element.143, f32[16,4,128]{2,1,0:T(4,128)S(1)} %bitcast.100, f32[16,128]{1,0:T(8,128)S(1)} %get-tuple-element.145, f32[16,4,128]{2,1,0:T(4,128)S(1)} %bitcast.99, ...), kind=kOutput, calls=%fused_computation.28.clone.1 | convolution fusion | flops 115343360 | bytes 458752 | tf_op jit(solution)/shard_map/while/body/eval_jaxpr/gkij,gkcj->gci/dot_general | solution.py:98
  88.5 2.8 %gather_fusion = f32[64,16,128]{2,1,0:T(8,128)S(1)} fusion(f32[512,16,128]{2,1,0:T(8,128)} %get-tuple-element.165, s32[1024]{0:T(1024)S(1)} %pad_clamp_fusion.3), kind=kCustom, calls=%fused_computation.clone.1 | custom fusion | bytes 1048832 | tf_op jit(solution)/shard_map/while/body/eval_jaxpr/gather | solution.py:96
  91.5 5.8 %fusion.52 = f32[1,16,8,128]{3,2,1,0:T(8,128)S(1)} fusion(f32[16,4]{1,0:T(8,128)S(1)} %copy.145, f32[16,4,128]{2,1,0:T(4,128)S(1)} %bitcast.101, f32[16,128]{1,0:T(8,128)S(1)} %get-tuple-element.143, f32[16,4,128]{2,1,0:T(4,128)S(1)} %bitcast.100, f32[16,128]{1,0:T(8,128)S(1)} %get-tuple-element.145, f32[16,4,128]{2,1,0:T(4,128)S(1)} %bitcast.99, ...), kind=kOutput, calls=%fused_computation.28.clone.1 | convolution fusion | flops 115343360 | bytes 458752 | tf_op jit(solution)/shard_map/while/body/eval_jaxpr/gkij,gkcj->gci/dot_general | solution.py:98
  98.2 2.8 %gather_fusion = f32[64,16,128]{2,1,0:T(8,128)S(1)} fusion(f32[512,16,128]{2,1,0:T(8,128)} %get-tuple-element.165, s32[1024]{0:T(1024)S(1)} %pad_clamp_fusion.3), kind=kCustom, calls=%fused_computation.clone.1 | custom fusion | bytes 1048832 | tf_op jit(solution)/shard_map/while/body/eval_jaxpr/gather | solution.py:96
  101.2 5.8 %fusion.52 = f32[1,16,8,128]{3,2,1,0:T(8,128)S(1)} fusion(f32[16,4]{1,0:T(8,128)S(1)} %copy.145, f32[16,4,128]{2,1,0:T(4,128)S(1)} %bitcast.101, f32[16,128]{1,0:T(8,128)S(1)} %get-tuple-element.143, f32[16,4,128]{2,1,0:T(4,128)S(1)} %bitcast.100, f32[16,128]{1,0:T(8,128)S(1)} %get-tuple-element.145, f32[16,4,128]{2,1,0:T(4,128)S(1)} %bitcast.99, ...), kind=kOutput, calls=%fused_computation.28.clone.1 | convolution fusion | flops 115343360 | bytes 458752 | tf_op jit(solution)/shard_map/while/body/eval_jaxpr/gkij,gkcj->gci/dot_general | solution.py:98
  107.8 2.8 %gather_fusion = f32[64,16,128]{2,1,0:T(8,128)S(1)} fusion(f32[512,16,128]{2,1,0:T(8,128)} %get-tuple-element.165, s32[1024]{0:T(1024)S(1)} %pad_clamp_fusion.3), kind=kCustom, calls=%fused_computation.clone.1 | custom fusion | bytes 1048832 | tf_op jit(solution)/shard_map/while/body/eval_jaxpr/gather | solution.py:96
  110.8 5.8 %fusion.52 = f32[1,16,8,128]{3,2,1,0:T(8,128)S(1)} fusion(f32[16,4]{1,0:T(8,128)S(1)} %copy.145, f32[16,4,128]{2,1,0:T(4,128)S(1)} %bitcast.101, f32[16,128]{1,0:T(8,128)S(1)} %get-tuple-element.143, f32[16,4,128]{2,1,0:T(4,128)S(1)} %bitcast.100, f32[16,128]{1,0:T(8,128)S(1)} %get-tuple-element.145, f32[16,4,128]{2,1,0:T(4,128)S(1)} %bitcast.99, ...), kind=kOutput, calls=%fused_computation.28.clone.1 | convolution fusion | flops 115343360 | bytes 458752 | tf_op jit(solution)/shard_map/while/body/eval_jaxpr/gkij,gkcj->gci/dot_general | solution.py:98
  117.5 2.8 %gather_fusion = f32[64,16,128]{2,1,0:T(8,128)S(1)} fusion(f32[512,16,128]{2,1,0:T(8,128)} %get-tuple-element.165, s32[1024]{0:T(1024)S(1)} %pad_clamp_fusion.3), kind=kCustom, calls=%fused_computation.clone.1 | custom fusion | bytes 1048832 | tf_op jit(solution)/shard_map/while/body/eval_jaxpr/gather | solution.py:96
  120.5 5.8 %fusion.52 = f32[1,16,8,128]{3,2,1,0:T(8,128)S(1)} fusion(f32[16,4]{1,0:T(8,128)S(1)} %copy.145, f32[16,4,128]{2,1,0:T(4,128)S(1)} %bitcast.101, f32[16,128]{1,0:T(8,128)S(1)} %get-tuple-element.143, f32[16,4,128]{2,1,0:T(4,128)S(1)} %bitcast.100, f32[16,128]{1,0:T(8,128)S(1)} %get-tuple-element.145, f32[16,4,128]{2,1,0:T(4,128)S(1)} %bitcast.99, ...), kind=kOutput, calls=%fused_computation.28.clone.1 | convolution fusion | flops 115343360 | bytes 458752 | tf_op jit(solution)/shard_map/while/body/eval_jaxpr/gkij,gkcj->gci/dot_general | solution.py:98
  127.1 2.8 %gather_fusion = f32[64,16,128]{2,1,0:T(8,128)S(1)} fusion(f32[512,16,128]{2,1,0:T(8,128)} %get-tuple-element.165, s32[1024]{0:T(1024)S(1)} %pad_clamp_fusion.3), kind=kCustom, calls=%fused_computation.clone.1 | custom fusion | bytes 1048832 | tf_op jit(solution)/shard_map/while/body/eval_jaxpr/gather | solution.py:96
  130.1 5.8 %fusion.52 = f32[1,16,8,128]{3,2,1,0:T(8,128)S(1)} fusion(f32[16,4]{1,0:T(8,128)S(1)} %copy.145, f32[16,4,128]{2,1,0:T(4,128)S(1)} %bitcast.101, f32[16,128]{1,0:T(8,128)S(1)} %get-tuple-element.143, f32[16,4,128]{2,1,0:T(4,128)S(1)} %bitcast.100, f32[16,128]{1,0:T(8,128)S(1)} %get-tuple-element.145, f32[16,4,128]{2,1,0:T(4,128)S(1)} %bitcast.99, ...), kind=kOutput, calls=%fused_computation.28.clone.1 | convolution fusion | flops 115343360 | bytes 458752 | tf_op jit(solution)/shard_map/while/body/eval_jaxpr/gkij,gkcj->gci/dot_general | solution.py:98
  136.7 2.8 %gather_fusion = f32[64,16,128]{2,1,0:T(8,128)S(1)} fusion(f32[512,16,128]{2,1,0:T(8,128)} %get-tuple-element.165, s32[1024]{0:T(1024)S(1)} %pad_clamp_fusion.3), kind=kCustom, calls=%fused_computation.clone.1 | custom fusion | bytes 1048832 | tf_op jit(solution)/shard_map/while/body/eval_jaxpr/gather | solution.py:96
  139.7 5.8 %fusion.52 = f32[1,16,8,128]{3,2,1,0:T(8,128)S(1)} fusion(f32[16,4]{1,0:T(8,128)S(1)} %copy.145, f32[16,4,128]{2,1,0:T(4,128)S(1)} %bitcast.101, f32[16,128]{1,0:T(8,128)S(1)} %get-tuple-element.143, f32[16,4,128]{2,1,0:T(4,128)S(1)} %bitcast.100, f32[16,128]{1,0:T(8,128)S(1)} %get-tuple-element.145, f32[16,4,128]{2,1,0:T(4,128)S(1)} %bitcast.99, ...), kind=kOutput, calls=%fused_computation.28.clone.1 | convolution fusion | flops 115343360 | bytes 458752 | tf_op jit(solution)/shard_map/while/body/eval_jaxpr/gkij,gkcj->gci/dot_general | solution.py:98
  146.4 2.8 %gather_fusion = f32[64,16,128]{2,1,0:T(8,128)S(1)} fusion(f32[512,16,128]{2,1,0:T(8,128)} %get-tuple-element.165, s32[1024]{0:T(1024)S(1)} %pad_clamp_fusion.3), kind=kCustom, calls=%fused_computation.clone.1 | custom fusion | bytes 1048832 | tf_op jit(solution)/shard_map/while/body/eval_jaxpr/gather | solution.py:96
  149.4 5.8 %fusion.52 = f32[1,16,8,128]{3,2,1,0:T(8,128)S(1)} fusion(f32[16,4]{1,0:T(8,128)S(1)} %copy.145, f32[16,4,128]{2,1,0:T(4,128)S(1)} %bitcast.101, f32[16,128]{1,0:T(8,128)S(1)} %get-tuple-element.143, f32[16,4,128]{2,1,0:T(4,128)S(1)} %bitcast.100, f32[16,128]{1,0:T(8,128)S(1)} %get-tuple-element.145, f32[16,4,128]{2,1,0:T(4,128)S(1)} %bitcast.99, ...), kind=kOutput, calls=%fused_computation.28.clone.1 | convolution fusion | flops 115343360 | bytes 458752 | tf_op jit(solution)/shard_map/while/body/eval_jaxpr/gkij,gkcj->gci/dot_general | solution.py:98
  156.0 2.8 %gather_fusion = f32[64,16,128]{2,1,0:T(8,128)S(1)} fusion(f32[512,16,128]{2,1,0:T(8,128)} %get-tuple-element.165, s32[1024]{0:T(1024)S(1)} %pad_clamp_fusion.3), kind=kCustom, calls=%fused_computation.clone.1 | custom fusion | bytes 1048832 | tf_op jit(solution)/shard_map/while/body/eval_jaxpr/gather | solution.py:96
  159.0 5.8 %fusion.52 = f32[1,16,8,128]{3,2,1,0:T(8,128)S(1)} fusion(f32[16,4]{1,0:T(8,128)S(1)} %copy.145, f32[16,4,128]{2,1,0:T(4,128)S(1)} %bitcast.101, f32[16,128]{1,0:T(8,128)S(1)} %get-tuple-element.143, f32[16,4,128]{2,1,0:T(4,128)S(1)} %bitcast.100, f32[16,128]{1,0:T(8,128)S(1)} %get-tuple-element.145, f32[16,4,128]{2,1,0:T(4,128)S(1)} %bitcast.99, ...), kind=kOutput, calls=%fused_computation.28.clone.1 | convolution fusion | flops 115343360 | bytes 458752 | tf_op jit(solution)/shard_map/while/body/eval_jaxpr/gkij,gkcj->gci/dot_general | solution.py:98
  165.7 2.8 %gather_fusion = f32[64,16,128]{2,1,0:T(8,128)S(1)} fusion(f32[512,16,128]{2,1,0:T(8,128)} %get-tuple-element.165, s32[1024]{0:T(1024)S(1)} %pad_clamp_fusion.3), kind=kCustom, calls=%fused_computation.clone.1 | custom fusion | bytes 1048832 | tf_op jit(solution)/shard_map/while/body/eval_jaxpr/gather | solution.py:96
  168.7 5.8 %fusion.52 = f32[1,16,8,128]{3,2,1,0:T(8,128)S(1)} fusion(f32[16,4]{1,0:T(8,128)S(1)} %copy.145, f32[16,4,128]{2,1,0:T(4,128)S(1)} %bitcast.101, f32[16,128]{1,0:T(8,128)S(1)} %get-tuple-element.143, f32[16,4,128]{2,1,0:T(4,128)S(1)} %bitcast.100, f32[16,128]{1,0:T(8,128)S(1)} %get-tuple-element.145, f32[16,4,128]{2,1,0:T(4,128)S(1)} %bitcast.99, ...), kind=kOutput, calls=%fused_computation.28.clone.1 | convolution fusion | flops 115343360 | bytes 458752 | tf_op jit(solution)/shard_map/while/body/eval_jaxpr/gkij,gkcj->gci/dot_general | solution.py:98
  175.3 2.8 %gather_fusion = f32[64,16,128]{2,1,0:T(8,128)S(1)} fusion(f32[512,16,128]{2,1,0:T(8,128)} %get-tuple-element.165, s32[1024]{0:T(1024)S(1)} %pad_clamp_fusion.3), kind=kCustom, calls=%fused_computation.clone.1 | custom fusion | bytes 1048832 | tf_op jit(solution)/shard_map/while/body/eval_jaxpr/gather | solution.py:96
  178.3 5.8 %fusion.52 = f32[1,16,8,128]{3,2,1,0:T(8,128)S(1)} fusion(f32[16,4]{1,0:T(8,128)S(1)} %copy.145, f32[16,4,128]{2,1,0:T(4,128)S(1)} %bitcast.101, f32[16,128]{1,0:T(8,128)S(1)} %get-tuple-element.143, f32[16,4,128]{2,1,0:T(4,128)S(1)} %bitcast.100, f32[16,128]{1,0:T(8,128)S(1)} %get-tuple-element.145, f32[16,4,128]{2,1,0:T(4,128)S(1)} %bitcast.99, ...), kind=kOutput, calls=%fused_computation.28.clone.1 | convolution fusion | flops 115343360 | bytes 458752 | tf_op jit(solution)/shard_map/while/body/eval_jaxpr/gkij,gkcj->gci/dot_general | solution.py:98
  185.0 2.8 %gather_fusion = f32[64,16,128]{2,1,0:T(8,128)S(1)} fusion(f32[512,16,128]{2,1,0:T(8,128)} %get-tuple-element.165, s32[1024]{0:T(1024)S(1)} %pad_clamp_fusion.3), kind=kCustom, calls=%fused_computation.clone.1 | custom fusion | bytes 1048832 | tf_op jit(solution)/shard_map/while/body/eval_jaxpr/gather | solution.py:96
  188.0 5.8 %fusion.52 = f32[1,16,8,128]{3,2,1,0:T(8,128)S(1)} fusion(f32[16,4]{1,0:T(8,128)S(1)} %copy.145, f32[16,4,128]{2,1,0:T(4,128)S(1)} %bitcast.101, f32[16,128]{1,0:T(8,128)S(1)} %get-tuple-element.143, f32[16,4,128]{2,1,0:T(4,128)S(1)} %bitcast.100, f32[16,128]{1,0:T(8,128)S(1)} %get-tuple-element.145, f32[16,4,128]{2,1,0:T(4,128)S(1)} %bitcast.99, ...), kind=kOutput, calls=%fused_computation.28.clone.1 | convolution fusion | flops 115343360 | bytes 458752 | tf_op jit(solution)/shard_map/while/body/eval_jaxpr/gkij,gkcj->gci/dot_general | solution.py:98
  194.6 2.8 %gather_fusion = f32[64,16,128]{2,1,0:T(8,128)S(1)} fusion(f32[512,16,128]{2,1,0:T(8,128)} %get-tuple-element.165, s32[1024]{0:T(1024)S(1)} %pad_clamp_fusion.3), kind=kCustom, calls=%fused_computation.clone.1 | custom fusion | bytes 1048832 | tf_op jit(solution)/shard_map/while/body/eval_jaxpr/gather | solution.py:96
  197.6 5.8 %fusion.52 = f32[1,16,8,128]{3,2,1,0:T(8,128)S(1)} fusion(f32[16,4]{1,0:T(8,128)S(1)} %copy.145, f32[16,4,128]{2,1,0:T(4,128)S(1)} %bitcast.101, f32[16,128]{1,0:T(8,128)S(1)} %get-tuple-element.143, f32[16,4,128]{2,1,0:T(4,128)S(1)} %bitcast.100, f32[16,128]{1,0:T(8,128)S(1)} %get-tuple-element.145, f32[16,4,128]{2,1,0:T(4,128)S(1)} %bitcast.99, ...), kind=kOutput, calls=%fused_computation.28.clone.1 | convolution fusion | flops 115343360 | bytes 458752 | tf_op jit(solution)/shard_map/while/body/eval_jaxpr/gkij,gkcj->gci/dot_general | solution.py:98
  206.6 8.7 %copy.131 = f32[256,12,128]{1,2,0:T(8,128)} copy(f32[256,12,128]{2,0,1:T(8,128)S(1)} %constant_dynamic-update-slice_fusion.4) | data formatting | bytes 3145728 | tf_op jit(solution)/shard_map/concatenate | solution.py:55
  215.3 10.5 %gather_fusion.2 = f32[1024,12]{1,0:T(8,128)S(1)} fusion(f32[256,12,128]{1,2,0:T(8,128)} %copy.131, s32[1024]{0:T(1024)S(1)} %bitcast.85), kind=kCustom, calls=%fused_computation.2 | custom fusion | bytes 106496 | tf_op jit(solution)/shard_map/gather | solution.py:124
  227.4 13.4 %all-to-all-start = ((f32[64,1,192]{2,1,0:T(1,128)}), f32[64,1,192]{2,1,0:T(1,128)S(1)}, u32[]{:S(2)}, u32[]{:S(2)}) async-start(f32[64,1,192]{2,1,0:T(1,128)} %reshape.291), calls=%async_computation | async-start | bytes 131072 | tf_op jit(solution)/shard_map/all_to_all | solution.py:126
  242.0 8.5 %all-to-all-done = f32[64,1,192]{2,1,0:T(1,128)S(1)} async-done(((f32[64,1,192]{2,1,0:T(1,128)}), f32[64,1,192]{2,1,0:T(1,128)S(1)}, u32[]{:S(2)}, u32[]{:S(2)}) %all-to-all-start) | async-done | bytes 49184 | tf_op jit(solution)/shard_map/all_to_all | solution.py:126
  (254 shorter events, 41.0 us)
Async XLA Ops:
  0.6 4.5 %copy-start = (f32[256,12,128]{2,0,1:T(8,128)S(1)}, f32[256,12,128]{2,0,1:T(8,128)}, u32[]{:S(2)}) copy-start(f32[256,12,128]{2,0,1:T(8,128)} %param.9) | copy-start | bytes 4718596
  6.6 3.0 %copy-start.5 = (s32[1,4,64]{2,1,0:T(4,128)S(1)}, s32[1,4,64]{2,1,0:T(4,128)}, u32[]{:S(2)}) copy-start(s32[1,4,64]{2,1,0:T(4,128)} %param.12) | copy-start | bytes 3076
  13.5 2.1 copy-start.7
  15.9 12.6 %copy-start.4 = (s32[256,4]{0,1:T(4,128)S(1)}, s32[256,4]{0,1:T(4,128)}, u32[]{:S(2)}) copy-start(s32[256,4]{0,1:T(4,128)} %param.11) | copy-start | bytes 12292
  15.9 12.6 %copy-start.3 = (s32[256,4]{0,1:T(4,128)S(1)}, s32[256,4]{0,1:T(4,128)}, u32[]{:S(2)}) copy-start(s32[256,4]{0,1:T(4,128)} %param.10) | copy-start | bytes 12292
  15.9 12.7 %copy-start.2 = (s32[1,64,16]{1,2,0:T(8,128)S(1)}, s32[1,64,16]{1,2,0:T(8,128)}, u32[]{:S(2)}) copy-start(s32[1,64,16]{1,2,0:T(8,128)} %param.14) | copy-start | bytes 12292
  15.9 12.9 %copy-start.6 = (s32[1,64]{1,0:T(1,128)S(1)}, s32[1,64]{1,0:T(1,128)}, u32[]{:S(2)}) copy-start(s32[1,64]{1,0:T(1,128)} %param.15) | copy-start | bytes 772
  15.9 13.1 %copy-start.9 = (s32[2]{0:T(128)S(1)}, s32[2]{0:T(128)}, u32[]{:S(2)}) copy-start(s32[2]{0:T(128)} %constant.88) | copy-start | bytes 28
  15.9 13.2 %copy-start.8 = (s32[2]{0:T(128)S(1)}, s32[2]{0:T(128)}, u32[]{:S(2)}) copy-start(s32[2]{0:T(128)} %constant.91) | copy-start | bytes 28
  17.1 18.2 %collective-permute-start = (f32[1,64,11,128]{3,1,2,0:T(8,128)}, f32[1,64,11,128]{3,1,2,0:T(8,128)}, u32[]{:S(2)}, u32[]{:S(2)}) collective-permute-start(f32[1,64,11,128]{3,1,2,0:T(8,128)} %get-tuple-element.98), channel_id=1, source_target_pairs={{0,1},{1,2},{2,3},{3,4},{4,5},{5,6},{6,7},{7,8},{8,9},{9,10},{10,1... | collective-permute-start | bytes 1081352 | tf_op jit(solution)/shard_map/ppermute | solution.py:14
  22.1 15.0 %collective-permute-start.1 = (f32[1,64,11,128]{3,1,2,0:T(8,128)}, f32[1,64,11,128]{3,1,2,0:T(8,128)}, u32[]{:S(2)}, u32[]{:S(2)}) collective-permute-start(f32[1,64,11,128]{3,1,2,0:T(8,128)} %get-tuple-element.97), channel_id=1, source_target_pairs={{1,0},{2,1},{3,2},{4,3},{5,4},{6,5},{7,6},{8,7},{9,8},{10,9},{11,1... | collective-permute-start | bytes 1081352 | tf_op jit(solution)/shard_map/ppermute | solution.py:15
  24.3 14.5 %collective-permute-start.2 = (f32[1,64,11,128]{3,1,2,0:T(8,128)}, f32[1,64,11,128]{3,1,2,0:T(8,128)S(1)}, u32[]{:S(2)}, u32[]{:S(2)}) collective-permute-start(f32[1,64,11,128]{3,1,2,0:T(8,128)} %get-tuple-element.96), channel_id=1, source_target_pairs={{0,64},{64,128},{128,192},{1,65},{65,129},{129,193},{2,66},{66,130... | collective-permute-start | bytes 1081352 | tf_op jit(solution)/shard_map/ppermute | solution.py:14
  27.1 12.5 %collective-permute-start.3 = (f32[1,64,11,128]{3,1,2,0:T(8,128)}, f32[1,64,11,128]{3,1,2,0:T(8,128)S(1)}, u32[]{:S(2)}, u32[]{:S(2)}) collective-permute-start(f32[1,64,11,128]{3,1,2,0:T(8,128)} %get-tuple-element.95), channel_id=1, source_target_pairs={{64,0},{128,64},{192,128},{65,1},{129,65},{193,129},{66,2},{130,66... | collective-permute-start | bytes 1081352 | tf_op jit(solution)/shard_map/ppermute | solution.py:15
  204.0 2.1 copy-start.1
  227.4 23.2 %all-to-all-start = ((f32[64,1,192]{2,1,0:T(1,128)}), f32[64,1,192]{2,1,0:T(1,128)S(1)}, u32[]{:S(2)}, u32[]{:S(2)}) async-start(f32[64,1,192]{2,1,0:T(1,128)} %reshape.291), calls=%async_computation | async-start | bytes 131072 | tf_op jit(solution)/shard_map/all_to_all | solution.py:126
where the time goes:
time: 255 us; the launch traced here: 253 us
  local copies, waits for them, and re-layouts  109 us (43%)
  matrix products  92.5 us (36%)
  starting transfers between devices  24.6 us (10%)
  other arithmetic  17 us (7%)
  waiting for transfers between devices  8.54 us (3%)
    dot_general x16, matrix products, one_group(): jnp.einsum('gkij,gkcj->gci', kernel_weight, nearby_particles[:, :, 8:16],...  92.5 us
    gather x16, local copies, waits for them, and re-layouts, one_group(): nearby_particles = table[nbr_group]  44.5 us
    all_to_all x1, starting transfers between devices, on_device(): lax.all_to_all(outbound, 'dom', split_axis=1, concat_axis=1, tiled=True)  13.4 us
    dynamic_update_slice x16, local copies, waits for them, and re-layouts, on_device(): lax.map(one_group, (own_pos.reshape(blocks // group, group, 3, 128), neig...  10.6 us
    gather x1, local copies, waits for them, and re-layouts, on_device(): leaving = updated[block_of, :, lane_of] * sending[:, None]  10.5 us
    unnamed x11, other arithmetic  9.89 us
    concatenate x2, local copies, waits for them, and re-layouts, advance(): jnp.concatenate([position_new, velocity_new, state[:, 6:7], sums[:, 0:1],...  8.74 us
    all_to_all x1, waiting for transfers between devices, on_device(): lax.all_to_all(outbound, 'dom', split_axis=1, concat_axis=1, tiled=True)  8.53 us
  transfers between devices with their start and end apart: 5, of which 1 were waited for; matrix products, arithmetic and copies ran while one was open for 5% of the time, Pallas kernels for 0%

commit v1 on v0

v1 whole, which is shorter than its diff:
```python
import functools

import jax
import jax.numpy as jnp
from jax import lax
from jax.experimental import pallas as pl
from jax.experimental.pallas import tpu as pltpu
from jax.sharding import PartitionSpec as P

MESH = pl.DeviceIdType.MESH
F32 = jnp.float32
BF16 = jnp.bfloat16
NB = 256
HB = 64
NC = 512
FR = 48
CR = 32
U = 8
REACH = 2.0
NT = (((1,), (1,)), ((), ()))
TN = (((0,), (0,)), ((), ()))
VMEM_LIMIT = 58 << 20


def carried_planes(st, rows):
    mass = st[6, rows, :]
    volume = mass / st[7, rows, :]
    out = [mass, volume]
    for ch in (8, 9, 10, 3, 4, 5):
        out.append(volume * st[ch, rows, :])
    return out


def exchange_kernel(lists, counts, st, halo_c, halo_x, tab_c, tab_x, send_c, pick_x, send_x, ssem, rsem):
    grp, dom = lax.axis_index("grp"), lax.axis_index("dom")
    n_grp, n_dom = lax.axis_size("grp"), lax.axis_size("dom")
    has = [dom > 0, dom < n_dom - 1, grp > 0, grp < n_grp - 1]
    peer = [(grp, dom - 1), (grp, dom + 1), (grp - 1, dom), (grp + 1, dom)]
    barrier = pltpu.get_barrier_semaphore()
    for p in range(4):

        @pl.when(has[p])
        def _(p=p):
            pl.semaphore_signal(barrier, inc=1, device_id=peer[p], device_id_type=MESH)

    def build(q, carry):
        rows = pl.ds(pl.multiple_of(q * 32, 32), 32)
        for c, plane in enumerate(carried_planes(st, rows)):
            tab_c[rows, c, :] = plane
        for c in range(3):
            tab_x[rows, c, :] = st[c, rows, :]
        return carry

    lax.fori_loop(0, NB // 32, build, 0)

    def copies(p):
        slot = p ^ 1
        return [
            pltpu.make_async_remote_copy(
                src_ref=send_c.at[pl.ds(p * HB * 8, HB * 8)],
                dst_ref=halo_c.at[pl.ds(slot * HB * 8, HB * 8)],
                send_sem=ssem.at[p, 0],
                recv_sem=rsem.at[slot, 0],
                device_id=peer[p],
                device_id_type=MESH,
            ),
            pltpu.make_async_remote_copy(
                src_ref=send_x.at[:, p],
                dst_ref=halo_x.at[:, slot],
                send_sem=ssem.at[p, 1],
                recv_sem=rsem.at[slot, 1],
                device_id=peer[p],
                device_id_type=MESH,
            ),
        ]

    met = False
    for p in (3, 2, 1, 0):

        def pick(t, carry, p=p):
            for u in range(8):
                s = t * 8 + u
                live = jnp.where(s < counts[0, p], 1.0, 0.0).astype(F32)
                b = lists[p, s]
                send_c[pl.ds(pl.multiple_of(p * HB * 8 + s * 8, 8), 8), :] = tab_c[b] * live
                pick_x[pl.ds(pl.multiple_of(s * 8, 8), 8), :] = tab_x[b] * live
            return carry

        lax.fori_loop(0, HB // 8, pick, 0)
        for c in range(3):
            send_x[c, p] = pick_x[pl.ds(c, HB, stride=8), :]
        if not met:
            pl.semaphore_wait(barrier, sum(h.astype(jnp.int32) for h in has))
            met = True

        @pl.when(has[p])
        def _(p=p):
            for copy in copies(p):
                copy.start()

    for p in range(4):

        @pl.when(jnp.logical_not(has[p]))
        def _(p=p):
            halo_c[pl.ds(p * HB * 8, HB * 8), :] = jnp.zeros((HB * 8, 128), F32)
            halo_x[:, p] = jnp.zeros((3, HB, 128), F32)

    for p in range(4):

        @pl.when(has[p])
        def _(p=p):
            for copy in copies(p):
                copy.wait_send()
            for copy in copies(p ^ 1):
                copy.wait_recv()


def exchange(lists, counts, planes):
    return pl.pallas_call(
        exchange_kernel,
        out_shape=(
            jax.ShapeDtypeStruct((4 * HB * 8, 128), F32),
            jax.ShapeDtypeStruct((3, 4, HB, 128), F32),
        ),
        in_specs=[
            pl.BlockSpec(memory_space=pltpu.SMEM),
            pl.BlockSpec(memory_space=pltpu.SMEM),
            pl.BlockSpec(memory_space=pltpu.VMEM),
        ],
        out_specs=(pl.BlockSpec(memory_space=pltpu.VMEM), pl.BlockSpec(memory_space=pltpu.VMEM)),
        scratch_shapes=[
            pltpu.VMEM((NB, 8, 128), F32),
            pltpu.VMEM((NB, 8, 128), F32),
            pltpu.VMEM((4 * HB * 8, 128), F32),
            pltpu.VMEM((HB * 8, 128), F32),
            pltpu.VMEM((3, 4, HB, 128), F32),
            pltpu.SemaphoreType.DMA((4, 2)),
            pltpu.SemaphoreType.DMA((4, 2)),
        ],
        compiler_params=pltpu.CompilerParams(
            collective_id=0, has_side_effects=True, vmem_limit_bytes=VMEM_LIMIT
        ),
    )(lists, counts, planes)


def swap_groups(v):
    row = lax.broadcasted_iota(jnp.int32, (8, 128), 0)
    group = lax.broadcasted_iota(jnp.int32, (8, 128), 1) // 16
    apart = (row - group) & 7
    out = v
    for d in range(1, 8):
        moved = pltpu.roll(pltpu.roll(v, d, 0), 128 - 16 * d, 1)
        out = jnp.where(apart == d, moved, out)
    return out


def pieces(v):
    first = v.astype(BF16).astype(F32)
    rest = v - first
    second = rest.astype(BF16).astype(F32)
    return first, second, rest - second


def local_kernel(
    nbr, mask, movers_s, counts_s, st, halo_c, halo_x, movers_v, counts_v, kept, message,
    tab_x, tab_p, tab_c, feat, own_feat, car, sums, upd, *stages,
):
    dist, high, low = stages[:U], stages[U : 2 * U], stages[2 * U :]
    centre, wide = [], None
    for c in range(3):
        plane = st[c]
        top, bottom = jnp.max(plane), jnp.min(plane)
        centre.append(0.5 * top + 0.5 * bottom)
        half = 0.5 * top - 0.5 * bottom
        wide = half if wide is None else jnp.maximum(wide, half)
    close = wide <= REACH

    def features(q, carry):
        own = pl.ds(pl.multiple_of(q * 32, 32), 32)
        zero, one = jnp.zeros((32, 128), F32), jnp.ones((32, 128), F32)
        for first in (0, NB):
            norm, xs = None, []
            for c in range(3):
                raw = st[c, own, :] if first == 0 else halo_x[c, own, :]
                x = jnp.clip(raw - centre[c], -REACH - 1.0, REACH + 1.0)
                norm = x * x if norm is None else norm + x * x
                xs.append(x)
            for c, plane in enumerate([*xs, 0.5 - norm, one, zero, zero, zero]):
                tab_x[pl.ds(first * 8 + q * 256 + c, 32, stride=8), :] = plane
            if first == 0:
                for c, plane in enumerate([*[2.0 * x for x in xs], one, -norm, zero, zero, zero]):
                    tab_p[pl.ds(q * 256 + c, 32, stride=8), :] = plane
        for c, plane in enumerate(carried_planes(st, own)):
            tab_c[pl.ds(q * 256 + c, 32, stride=8), :] = plane
        return carry

    lax.fori_loop(0, NB // 32, features, 0)

    def convert(q, carry):
        for u in range(8):
            b = q * 8 + u
            at = pl.ds(pl.multiple_of(b * 8, 8), 8)
            for n, own in ((b, True), (b + NB, False)):
                x1, x2, x3 = pieces(tab_x[pl.ds(pl.multiple_of(n * 8, 8), 8), :])
                feat[n] = jnp.concatenate([x1, x2, x3, x1, x2, x1], 0).astype(BF16)
                c1, c2, c3 = pieces(tab_c[at, :] if own else halo_c[at, :])
                car[n] = jnp.concatenate([c1, c2, c3, jnp.zeros_like(c1)], 0).astype(BF16)
            p1, p2, p3 = pieces(tab_p[at, :])
            own_feat[b] = jnp.concatenate([p1, p1, p1, p2, p2, p3], 0).astype(BF16)
        return carry

    lax.fori_loop(0, NB // 8, convert, 0)
    feat[NC] = jnp.zeros((FR, 128), BF16)
    car[NC] = jnp.zeros((CR, 128), BF16)

    def slot(k, i):
        return jnp.where(mask[k, i] == 0, NC, nbr[k, i])

    def store_sums(i, r):
        sums[pl.ds(pl.multiple_of(i * 8, 8), 8), :] = r[0:8] + r[8:16] + r[16:24]

    def split(w):
        h = w.astype(BF16)
        return h, (w - h.astype(F32)).astype(BF16)

    def measure(i, u):
        for half in range(2):
            near = jnp.concatenate([feat[slot(2 * half + k, i)] for k in range(2)], 1)
            dist[u][:, half * 256 : half * 256 + 256] = lax.dot_general(
                own_feat[i], near, TN, preferred_element_type=F32
            )

    def weigh(u):
        for half in range(2):
            cols = slice(half * 256, half * 256 + 256)
            s = jnp.maximum(dist[u][:, cols], 0.0)
            h, rest = split(s * s * s)
            high[u][:, cols] = h
            low[u][:, cols] = rest

    def contract(i, u):
        c = jnp.concatenate([car[slot(k, i)] for k in range(4)], 1)
        r = lax.dot_general(c, high[u][...], NT, preferred_element_type=F32)
        r = r + lax.dot_general(c, low[u][...], NT, preferred_element_type=F32)
        store_sums(i, r)

    @pl.when(close)
    def _():
        def body(t, carry):
            for u in range(U):
                i = t * U + u
                contract(jnp.maximum(i - 2, 0), (u - 2) % U)
                weigh((u - 1) % U)
                measure(i, u)
            return carry

        lax.fori_loop(0, NB // U, body, 0)
        contract(NB - 2, U - 2)
        weigh(U - 1)
        contract(NB - 1, U - 1)

    @pl.when(jnp.logical_not(close))
    def _():
        def raw(q, carry):
            own = pl.ds(pl.multiple_of(q * 32, 32), 32)
            for c in range(3):
                tab_x[pl.ds(q * 256 + c, 32, stride=8), :] = st[c, own, :]
                tab_x[pl.ds(NB * 8 + q * 256 + c, 32, stride=8), :] = halo_x[c, own, :]
            return carry

        lax.fori_loop(0, NB // 32, raw, 0)

        def body(i, carry):
            columns = jnp.transpose(tab_x[pl.ds(pl.multiple_of(i * 8, 8), 8), :])

            def pair(k, total):
                near = tab_x[pl.ds(pl.multiple_of(nbr[k, i] * 8, 8), 8), :]
                s = jnp.full((128, 128), 0.5, F32)
                for c in range(3):
                    delta = columns[:, c : c + 1] - near[c : c + 1, :]
                    s = s - delta * delta
                s = jnp.maximum(s, 0.0)
                h, rest = split(s * s * s)
                cc = car[slot(k, i)]
                r = lax.dot_general(cc, h, NT, preferred_element_type=F32)
                return total + r + lax.dot_general(cc, rest, NT, preferred_element_type=F32)

            store_sums(i, lax.fori_loop(0, 4, pair, jnp.zeros((CR, 128), F32)))
            return carry

        lax.fori_loop(0, NB, body, 0)

    mv = movers_v[...]
    per = mv.shape[0]
    slot_of = lax.broadcasted_iota(jnp.int32, mv.shape, 0)
    live = slot_of < counts_v[...]
    block_of = jnp.where(live, mv // 128, -1)
    lane_of = mv % 128
    gone = jnp.zeros((NB, 128), F32)
    for r in range(0, per, 2):
        b = jnp.concatenate([block_of[r : r + 1], block_of[r + 1 : r + 2]], 1)
        ln = jnp.concatenate([lane_of[r : r + 1], lane_of[r + 1 : r + 2]], 1)
        in_block = (lax.broadcasted_iota(jnp.int32, (NB, 128), 0) == b).astype(F32).astype(BF16)
        in_lane = (lax.broadcasted_iota(jnp.int32, (128, 128), 0) == ln).astype(F32).astype(BF16)
        gone = gone + lax.dot_general(in_block, in_lane, NT, preferred_element_type=F32)
    kept[0] = 1.0 - gone

    def advance(q, carry):
        rows = pl.ds(pl.multiple_of(q * 32, 32), 32)
        total = [8.0 * sums[pl.ds(q * 256 + c, 32, stride=8), :] for c in range(8)]
        position = [st[c, rows, :] for c in range(3)]
        velocity = [st[3 + c, rows, :] for c in range(3)]
        temper, one, two, solid = (st[c, rows, :] for c in range(8, 12))
        vol = total[1]
        temp_one = temper + 0.25 * (total[2] - temper * vol)
        conc_one = one + 0.2 * (total[3] - one * vol)
        conc_two = two + 0.1 * (total[4] - two * vol)
        v_new = [velocity[c] + 0.3 * (total[5 + c] - velocity[c] * vol) for c in range(3)]
        x_new = [position[c] + 0.02 * v_new[c] for c in range(3)]
        liquidus = 1.0 - 0.3 * conc_one - 0.2 * conc_two
        solid_new = jnp.maximum(solid, jnp.clip(2.0 * (liquidus - temp_one), 0.0, 1.0))
        temp_two = temp_one + 0.4 * (solid_new - solid)
        one_new = conc_one * (1.0 - 0.83 * solid) / (1.0 - 0.83 * solid_new)
        two_new = conc_two * (1.0 - 0.6 * solid) / (1.0 - 0.6 * solid_new)
        updated = [*x_new, *v_new, st[6, rows, :], total[0], temp_two, one_new, two_new, solid_new]
        stay = kept[0, rows, :]
        for c, plane in enumerate(updated):
            kept[c, rows, :] = plane * stay
            upd[pl.ds(q * 512 + c, 32, stride=16), :] = plane
        zero = jnp.zeros((32, 128), F32)
        for c in range(12, 16):
            upd[pl.ds(q * 512 + c, 32, stride=16), :] = zero
        return carry

    lax.fori_loop(0, NB // 32, advance, 0)

    upd[pl.ds(NB * 16, 16), :] = jnp.zeros((16, 128), F32)
    lane = lax.broadcasted_iota(jnp.int32, (16, 128), 1)

    def gather(g, carry):
        acc = jnp.zeros((16, 128), F32)
        for t in range(128):
            m = movers_s[t % 16, g * 8 + t // 16]
            b, ln = lax.shift_right_logical(m, 7), m & 127
            b = jnp.where(t % 16 < counts_s[0, g * 8 + t // 16], b, NB)
            v = upd[pl.ds(pl.multiple_of(b * 16, 16), 16), :]
            acc = jnp.where(lane == t, pltpu.roll(v, (t - ln) & 127, 1), acc)
        for h in range(2):
            message[pl.ds(g * 16 + h, 8, stride=2), :] = swap_groups(acc[8 * h : 8 * h + 8])
        return carry

    lax.fori_loop(0, movers_s.shape[1] // 8, gather, 0)


def local_step(nbr, mask, movers, planes, halo_c, halo_x, counts):
    smem, vmem = pl.BlockSpec(memory_space=pltpu.SMEM), pl.BlockSpec(memory_space=pltpu.VMEM)
    doms = movers.shape[1]
    return pl.pallas_call(
        local_kernel,
        out_shape=(
            jax.ShapeDtypeStruct((12, NB, 128), F32),
            jax.ShapeDtypeStruct((2 * doms, 128), F32),
        ),
        in_specs=[smem, smem, smem, smem, vmem, vmem, vmem, vmem, vmem],
        out_specs=(vmem, vmem),
        scratch_shapes=[
            pltpu.VMEM((NC * 8, 128), F32),
            pltpu.VMEM((NB * 8, 128), F32),
            pltpu.VMEM((NB * 8, 128), F32),
            pltpu.VMEM((NC + 1, FR, 128), BF16),
            pltpu.VMEM((NB, FR, 128), BF16),
            pltpu.VMEM((NC + 1, CR, 128), BF16),
            pltpu.VMEM((NB * 8, 128), F32),
            pltpu.VMEM((NB * 16 + 16, 128), F32),
            *[pltpu.VMEM((128, 512), F32)] * U,
            *[pltpu.VMEM((128, 512), BF16)] * (2 * U),
        ],
        compiler_params=pltpu.CompilerParams(vmem_limit_bytes=VMEM_LIMIT),
    )(nbr, mask, movers, counts, planes, halo_c, halo_x, movers, counts)


def migrate_kernel(doms, message, out, landed, ssem, rsem):
    grp, me = lax.axis_index("grp"), lax.axis_index("dom")
    barrier = pltpu.get_barrier_semaphore()

    def greet(k, carry):
        other = lax.rem(me + k, doms)
        pl.semaphore_signal(barrier, inc=1, device_id=(grp, other), device_id_type=MESH)
        return carry

    lax.fori_loop(1, doms, greet, 0)
    landed[me] = message[me]
    pl.semaphore_wait(barrier, doms - 1)

    def copy(k):
        other = lax.rem(me + k, doms)
        return pltpu.make_async_remote_copy(
            src_ref=message.at[other],
            dst_ref=landed.at[me],
            send_sem=ssem.at[k],
            recv_sem=rsem.at[k],
            device_id=(grp, other),
            device_id_type=MESH,
        )

    def send(k, carry):
        copy(k).start()
        return carry

    def finish(k, carry):
        copy(k).wait()
        return carry

    lax.fori_loop(1, doms, send, 0)
    lax.fori_loop(1, doms, finish, 0)
    for g in range(doms // 8):
        cols = slice(g * 128, g * 128 + 128)
        for h in range(2):
            rows = 8 if h == 0 else 4
            v = swap_groups(landed[pl.ds(g * 8, 8), h, :])
            out[8 * h : 8 * h + rows, cols] = v[:rows]


def migrate(message):
    doms = message.shape[0]
    vmem = pl.BlockSpec(memory_space=pltpu.VMEM)
    return pl.pallas_call(
        functools.partial(migrate_kernel, doms),
        out_shape=jax.ShapeDtypeStruct((12, doms * 16), F32),
        in_specs=[vmem],
        out_specs=vmem,
        scratch_shapes=[
            pltpu.VMEM((doms, 2, 128), F32),
            pltpu.SemaphoreType.DMA((doms,)),
            pltpu.SemaphoreType.DMA((doms,)),
        ],
        compiler_params=pltpu.CompilerParams(collective_id=1, has_side_effects=True),
    )(message)


def on_device(state, neighbours, pair_mask, send_lists, send_counts, movers, mover_counts):
    planes = state.transpose(1, 0, 2)
    halo_c, halo_x = exchange(send_lists[0], send_counts, planes)
    kept, message = local_step(
        neighbours.T, pair_mask.T, movers[0].T, planes, halo_c, halo_x.reshape(3, 4 * HB, 128), mover_counts
    )
    arrivals = migrate(message.reshape(-1, 2, 128))
    return kept.transpose(1, 0, 2), arrivals


def solution(mesh):
    both = ("grp", "dom")
    placed = (P(both, None, None), P(both, None), P(both, None), P(both, None, None), P(both, None), P(both, None, None), P(both, None))
    return jax.shard_map(
        on_device,
        mesh=mesh,
        in_specs=placed,
        out_specs=(P(both, None, None), P(None, both)),
        check_vma=False,
    )
```

time: 255 us -> 77.8 us (0.31)
  local copies, waits for them, and re-layouts: 109 us -> 1.47 us
  matrix products: 92.5 us -> 0 us
  Pallas kernels: 0 us -> 75.5 us
  starting transfers between devices: 24.6 us -> 0 us
  other arithmetic: 17 us -> 0 us
  waiting for transfers between devices: 8.54 us -> 0 us
    dot_general x16 -> x0, matrix products: 92.5 us -> none  [one_group(): jnp.einsum('gkij,gkcj->gci', kernel_weight, nearby_particles[:, :, 8:16],...]
    pallas_call x0 -> x3, Pallas kernels: none -> 75.5 us  [the longest x1 42.2 us: local_step(): pl.pallas_call(local_kernel, out_shape=(jax.ShapeDtypeStruct((12, NB, 128...]
    gather x19 -> x0, local copies, waits for them, and re-layouts: 60.8 us -> none  [the longest x16 44.5 us: one_group(): nearby_particles = table[nbr_group]]
    all_to_all x1 -> x0, starting transfers between devices: 13.4 us -> none  [on_device(): lax.all_to_all(outbound, 'dom', split_axis=1, concat_axis=1, tiled=True)]
    concatenate x6 -> x0, local copies, waits for them, and re-layouts: 12.6 us -> none  [the longest x2 8.74 us: advance(): jnp.concatenate([position_new, velocity_new, state[:, 6:7], sums[:, 0:1],...]
    ppermute x4 -> x0, starting transfers between devices: 11.3 us -> none  [the longest x2 7.73 us: with_halo(): before = lax.ppermute(last, axis, up)]
    dynamic_update_slice x16 -> x0, local copies, waits for them, and re-layouts: 10.6 us -> none  [on_device(): lax.map(one_group, (own_pos.reshape(blocks // group, group, 3, 128), neig...]
    unnamed x11 -> x0, other arithmetic: 9.89 us -> none
  transfers between devices with their start and end apart: 5 -> 0, of which waited for: 1 -> 0; matrix products, arithmetic and copies ran while one was open for 5% -> 0% of each run, Pallas kernels for 0% -> 0%
where the time goes in v1:
time: 77.8 us; the launch traced here: 77.6 us
  Pallas kernels  75.5 us (97%)
  local copies, waits for them, and re-layouts  1.47 us (2%)
    pallas_call x1, Pallas kernels, local_step(): pl.pallas_call(local_kernel, out_shape=(jax.ShapeDtypeStruct((12, NB, 128...  42.2 us
    pallas_call x1, Pallas kernels, migrate(): pl.pallas_call(functools.partial(migrate_kernel, doms), out_shape=jax.Sha...  17.9 us
    pallas_call x1, Pallas kernels, exchange(): pl.pallas_call(exchange_kernel, out_shape=(jax.ShapeDtypeStruct((4 * HB *...  15.4 us

profile of v1, /device:TPU:1, one launch (start us, length us, event | category | flops | bytes accessed | tf_op | source)
XLA Modules:
  0.0 77.6 jit_solution(7614928024003194670)
XLA Ops:
  0.6 15.4 %shard_map.86 = (f32[2048,128]{1,0:T(8,128)}, f32[3,4,64,128]{3,2,1,0:T(8,128)}) custom-call(s32[4,64]{1,0:T(4,128)} %bitcast.18, s32[1,4]{1,0:T(1,128)} %counts.1, f32[12,256,128]{2,1,0:T(8,128)} %bitcast.10), custom_call_target="tpu_custom_call" | custom-call | tf_op jit(solution)/shard_map/pallas_call | solution.py:119
  16.0 42.2 %shard_map.87 = (f32[12,256,128]{2,1,0:T(8,128)}, f32[128,128]{1,0:T(8,128)}) custom-call(s32[4,256]{1,0:T(4,128)} %bitcast.16, s32[4,256]{1,0:T(4,128)} %bitcast.17, s32[16,64]{1,0:T(8,128)} %bitcast.14, s32[1,64]{1,0:T(1,128)} %counts_v.1, f32[12,256,128]{2,1,0:T(8,128)} %bitcast.11, f32[2048,128]{1,0:T(8,128)} %get-tuple-element.6.halo_c, ...), custom_call_target="tpu_custom_call" | custom-call | tf_op jit(solution)/shard_map/pallas_call | solution.py:358
  58.2 17.9 %shard_map.88 = f32[12,1024]{1,0:T(8,128)} custom-call(f32[64,2,128]{2,1,0:T(2,128)} %bitcast.13), custom_call_target="tpu_custom_call" | custom-call | tf_op jit(solution)/shard_map/pallas_call | solution.py:427
  76.1 1.5 %copy.10 = f32[12,1024]{1,0:T(8,128)} copy(f32[12,1024]{1,0:T(8,128)} %shard_map.88) | data formatting | bytes 98304

commit v2 on v1

--- a/solution.py
+++ b/solution.py
@@ -1,5 +1,3 @@
-import functools
-
 import jax
 import jax.numpy as jnp
 from jax import lax
@@ -19,7 +17,7 @@
 REACH = 2.0
 NT = (((1,), (1,)), ((), ()))
 TN = (((0,), (0,)), ((), ()))
-VMEM_LIMIT = 58 << 20
+VMEM_LIMIT = 40 << 20
 
 
 def carried_planes(st, rows):
@@ -31,7 +29,17 @@
     return out
 
 
-def exchange_kernel(lists, counts, st, halo_c, halo_x, tab_c, tab_x, send_c, pick_x, send_x, ssem, rsem):
+def pieces(v):
+    first = v.astype(BF16).astype(F32)
+    rest = v - first
+    second = rest.astype(BF16).astype(F32)
+    return first, second, rest - second
+
+
+def exchange_kernel(
+    lists, counts, st, movers, mover_counts, halo_x, feat, own_feat, car, stay,
+    halo_c, tab_c, tab_x, near_x, tab_p, send_c, pick_x, send_x, ssem, rsem,
+):
     grp, dom = lax.axis_index("grp"), lax.axis_index("dom")
     n_grp, n_dom = lax.axis_size("grp"), lax.axis_size("dom")
     has = [dom > 0, dom < n_dom - 1, grp > 0, grp < n_grp - 1]
@@ -66,7 +74,7 @@
             ),
             pltpu.make_async_remote_copy(
                 src_ref=send_x.at[:, p],
-                dst_ref=halo_x.at[:, slot],
+                dst_ref=halo_x.at[:, pl.ds(slot * HB, HB)],
                 send_sem=ssem.at[p, 1],
                 recv_sem=rsem.at[slot, 1],
                 device_id=peer[p],
@@ -103,7 +111,63 @@
         @pl.when(jnp.logical_not(has[p]))
         def _(p=p):
             halo_c[pl.ds(p * HB * 8, HB * 8), :] = jnp.zeros((HB * 8, 128), F32)
-            halo_x[:, p] = jnp.zeros((3, HB, 128), F32)
+            halo_x[:, pl.ds(p * HB, HB), :] = jnp.zeros((3, HB, 128), F32)
+
+    centre = [0.5 * jnp.max(st[c]) + 0.5 * jnp.min(st[c]) for c in range(3)]
+
+    def features(source, own):
+        def body(q, carry):
+            rows = pl.ds(pl.multiple_of(q * 32, 32), 32)
+            zero, one = jnp.zeros((32, 128), F32), jnp.ones((32, 128), F32)
+            norm, xs = None, []
+            for c in range(3):
+                x = jnp.clip(source[c, rows, :] - centre[c], -REACH - 1.0, REACH + 1.0)
+                norm = x * x if norm is None else norm + x * x
+                xs.append(x)
+            for c, plane in enumerate([*xs, 0.5 - norm, one, zero, zero, zero]):
+                near_x[pl.ds(q * 256 + c, 32, stride=8), :] = plane
+            if own:
+                for c, plane in enumerate([*[2.0 * x for x in xs], one, -norm, zero, zero, zero]):
+                    tab_p[pl.ds(q * 256 + c, 32, stride=8), :] = plane
+            return carry
+
+        lax.fori_loop(0, NB // 32, body, 0)
+
+    def convert(own):
+        def body(q, carry):
+            for u in range(8):
+                b = q * 8 + u
+                at = pl.ds(pl.multiple_of(b * 8, 8), 8)
+                n = b if own else b + NB
+                x1, x2, x3 = pieces(near_x[at, :])
+                feat[n] = jnp.concatenate([x1, x2, x3, x1, x2, x1], 0).astype(BF16)
+                c1, c2, c3 = pieces(tab_c[b] if own else halo_c[at, :])
+                car[n] = jnp.concatenate([c1, c2, c3, jnp.zeros_like(c1)], 0).astype(BF16)
+                if own:
+                    p1, p2, p3 = pieces(tab_p[at, :])
+                    own_feat[b] = jnp.concatenate([p1, p1, p1, p2, p2, p3], 0).astype(BF16)
+            return carry
+
+        lax.fori_loop(0, NB // 8, body, 0)
+
+    features(st, True)
+    convert(True)
+    feat[NC] = jnp.zeros((FR, 128), BF16)
+    car[NC] = jnp.zeros((CR, 128), BF16)
+
+    mv = movers[...]
+    per = mv.shape[0]
+    live = lax.broadcasted_iota(jnp.int32, mv.shape, 0) < mover_counts[...]
+    block_of = jnp.where(live, lax.shift_right_logical(mv, 7), -1)
+    lane_of = mv & 127
+    gone = jnp.zeros((NB, 128), F32)
+    for r in range(0, per, 2):
+        b = jnp.concatenate([block_of[r : r + 1], block_of[r + 1 : r + 2]], 1)
+        ln = jnp.concatenate([lane_of[r : r + 1], lane_of[r + 1 : r + 2]], 1)
+        in_block = (lax.broadcasted_iota(jnp.int32, (NB, 128), 0) == b).astype(F32).astype(BF16)
+        in_lane = (lax.broadcasted_iota(jnp.int32, (128, 128), 0) == ln).astype(F32).astype(BF16)
+        gone = gone + lax.dot_general(in_block, in_lane, NT, preferred_element_type=F32)
+    stay[...] = 1.0 - gone
 
     for p in range(4):
 
@@ -114,23 +178,29 @@
             for copy in copies(p ^ 1):
                 copy.wait_recv()
 
-
-def exchange(lists, counts, planes):
+    features(halo_x, False)
+    convert(False)
+
+
+def exchange(lists, counts, planes, movers, mover_counts):
+    smem, vmem = pl.BlockSpec(memory_space=pltpu.SMEM), pl.BlockSpec(memory_space=pltpu.VMEM)
     return pl.pallas_call(
         exchange_kernel,
         out_shape=(
-            jax.ShapeDtypeStruct((4 * HB * 8, 128), F32),
-            jax.ShapeDtypeStruct((3, 4, HB, 128), F32),
+            pltpu.VMEM((3, 4 * HB, 128), F32),
+            pltpu.VMEM((NC + 1, FR, 128), BF16),
+            pltpu.VMEM((NB, FR, 128), BF16),
+            pltpu.VMEM((NC + 1, CR, 128), BF16),
+            pltpu.VMEM((NB, 128), F32),
         ),
-        in_specs=[
-            pl.BlockSpec(memory_space=pltpu.SMEM),
-            pl.BlockSpec(memory_space=pltpu.SMEM),
-            pl.BlockSpec(memory_space=pltpu.VMEM),
-        ],
-        out_specs=(pl.BlockSpec(memory_space=pltpu.VMEM), pl.BlockSpec(memory_space=pltpu.VMEM)),
+        in_specs=[smem, smem, vmem, vmem, vmem],
+        out_specs=(vmem,) * 5,
         scratch_shapes=[
+            pltpu.VMEM((4 * HB * 8, 128), F32),
             pltpu.VMEM((NB, 8, 128), F32),
             pltpu.VMEM((NB, 8, 128), F32),
+            pltpu.VMEM((NB * 8, 128), F32),
+            pltpu.VMEM((NB * 8, 128), F32),
             pltpu.VMEM((4 * HB * 8, 128), F32),
             pltpu.VMEM((HB * 8, 128), F32),
             pltpu.VMEM((3, 4, HB, 128), F32),
@@ -140,7 +210,7 @@
         compiler_params=pltpu.CompilerParams(
             collective_id=0, has_side_effects=True, vmem_limit_bytes=VMEM_LIMIT
         ),
-    )(lists, counts, planes)
+    )(lists, counts, planes, movers, mover_counts)
 
 
 def swap_groups(v):
@@ -154,64 +224,16 @@
     return out
 
 
-def pieces(v):
-    first = v.astype(BF16).astype(F32)
-    rest = v - first
-    second = rest.astype(BF16).astype(F32)
-    return first, second, rest - second
-
-
 def local_kernel(
-    nbr, mask, movers_s, counts_s, st, halo_c, halo_x, movers_v, counts_v, kept, message,
-    tab_x, tab_p, tab_c, feat, own_feat, car, sums, upd, *stages,
+    nbr, mask, movers_s, counts_s, st, halo_x, feat, own_feat, car, stay_ref, kept, message,
+    tab_x, sums, upd, *stages,
 ):
     dist, high, low = stages[:U], stages[U : 2 * U], stages[2 * U :]
-    centre, wide = [], None
+    wide = None
     for c in range(3):
-        plane = st[c]
-        top, bottom = jnp.max(plane), jnp.min(plane)
-        centre.append(0.5 * top + 0.5 * bottom)
-        half = 0.5 * top - 0.5 * bottom
+        half = 0.5 * jnp.max(st[c]) - 0.5 * jnp.min(st[c])
         wide = half if wide is None else jnp.maximum(wide, half)
     close = wide <= REACH
-
-    def features(q, carry):
-        own = pl.ds(pl.multiple_of(q * 32, 32), 32)
-        zero, one = jnp.zeros((32, 128), F32), jnp.ones((32, 128), F32)
-        for first in (0, NB):
-            norm, xs = None, []
-            for c in range(3):
-                raw = st[c, own, :] if first == 0 else halo_x[c, own, :]
-                x = jnp.clip(raw - centre[c], -REACH - 1.0, REACH + 1.0)
-                norm = x * x if norm is None else norm + x * x
-                xs.append(x)
-            for c, plane in enumerate([*xs, 0.5 - norm, one, zero, zero, zero]):
-                tab_x[pl.ds(first * 8 + q * 256 + c, 32, stride=8), :] = plane
-            if first == 0:
-                for c, plane in enumerate([*[2.0 * x for x in xs], one, -norm, zero, zero, zero]):
-                    tab_p[pl.ds(q * 256 + c, 32, stride=8), :] = plane
-        for c, plane in enumerate(carried_planes(st, own)):
-            tab_c[pl.ds(q * 256 + c, 32, stride=8), :] = plane
-        return carry
-
-    lax.fori_loop(0, NB // 32, features, 0)
-
-    def convert(q, carry):
-        for u in range(8):
-            b = q * 8 + u
-            at = pl.ds(pl.multiple_of(b * 8, 8), 8)
-            for n, own in ((b, True), (b + NB, False)):
-                x1, x2, x3 = pieces(tab_x[pl.ds(pl.multiple_of(n * 8, 8), 8), :])
-                feat[n] = jnp.concatenate([x1, x2, x3, x1, x2, x1], 0).astype(BF16)
-                c1, c2, c3 = pieces(tab_c[at, :] if own else halo_c[at, :])
-                car[n] = jnp.concatenate([c1, c2, c3, jnp.zeros_like(c1)], 0).astype(BF16)
-            p1, p2, p3 = pieces(tab_p[at, :])
-            own_feat[b] = jnp.concatenate([p1, p1, p1, p2, p2, p3], 0).astype(BF16)
-        return carry
-
-    lax.fori_loop(0, NB // 8, convert, 0)
-    feat[NC] = jnp.zeros((FR, 128), BF16)
-    car[NC] = jnp.zeros((CR, 128), BF16)
 
     def slot(k, i):
         return jnp.where(mask[k, i] == 0, NC, nbr[k, i])
@@ -289,21 +311,6 @@
             return carry
 
         lax.fori_loop(0, NB, body, 0)
-
-    mv = movers_v[...]
-    per = mv.shape[0]
-    slot_of = lax.broadcasted_iota(jnp.int32, mv.shape, 0)
-    live = slot_of < counts_v[...]
-    block_of = jnp.where(live, mv // 128, -1)
-    lane_of = mv % 128
-    gone = jnp.zeros((NB, 128), F32)
-    for r in range(0, per, 2):
-        b = jnp.concatenate([block_of[r : r + 1], block_of[r + 1 : r + 2]], 1)
-        ln = jnp.concatenate([lane_of[r : r + 1], lane_of[r + 1 : r + 2]], 1)
-        in_block = (lax.broadcasted_iota(jnp.int32, (NB, 128), 0) == b).astype(F32).astype(BF16)
-        in_lane = (lax.broadcasted_iota(jnp.int32, (128, 128), 0) == ln).astype(F32).astype(BF16)
-        gone = gone + lax.dot_general(in_block, in_lane, NT, preferred_element_type=F32)
-    kept[0] = 1.0 - gone
 
     def advance(q, carry):
         rows = pl.ds(pl.multiple_of(q * 32, 32), 32)
@@ -323,7 +330,7 @@
         one_new = conc_one * (1.0 - 0.83 * solid) / (1.0 - 0.83 * solid_new)
         two_new = conc_two * (1.0 - 0.6 * solid) / (1.0 - 0.6 * solid_new)
         updated = [*x_new, *v_new, st[6, rows, :], total[0], temp_two, one_new, two_new, solid_new]
-        stay = kept[0, rows, :]
+        stay = stay_ref[rows, :]
         for c, plane in enumerate(updated):
             kept[c, rows, :] = plane * stay
             upd[pl.ds(q * 512 + c, 32, stride=16), :] = plane
@@ -352,99 +359,119 @@
     lax.fori_loop(0, movers_s.shape[1] // 8, gather, 0)
 
 
-def local_step(nbr, mask, movers, planes, halo_c, halo_x, counts):
+def local_step(nbr, mask, movers, counts, planes, tables):
     smem, vmem = pl.BlockSpec(memory_space=pltpu.SMEM), pl.BlockSpec(memory_space=pltpu.VMEM)
     doms = movers.shape[1]
     return pl.pallas_call(
         local_kernel,
         out_shape=(
             jax.ShapeDtypeStruct((12, NB, 128), F32),
-            jax.ShapeDtypeStruct((2 * doms, 128), F32),
+            pltpu.VMEM((2 * doms, 128), F32),
         ),
-        in_specs=[smem, smem, smem, smem, vmem, vmem, vmem, vmem, vmem],
+        in_specs=[smem] * 4 + [vmem] * 6,
         out_specs=(vmem, vmem),
         scratch_shapes=[
             pltpu.VMEM((NC * 8, 128), F32),
-            pltpu.VMEM((NB * 8, 128), F32),
-            pltpu.VMEM((NB * 8, 128), F32),
-            pltpu.VMEM((NC + 1, FR, 128), BF16),
-            pltpu.VMEM((NB, FR, 128), BF16),
-            pltpu.VMEM((NC + 1, CR, 128), BF16),
             pltpu.VMEM((NB * 8, 128), F32),
             pltpu.VMEM((NB * 16 + 16, 128), F32),
             *[pltpu.VMEM((128, 512), F32)] * U,
             *[pltpu.VMEM((128, 512), BF16)] * (2 * U),
         ],
         compiler_params=pltpu.CompilerParams(vmem_limit_bytes=VMEM_LIMIT),
-    )(nbr, mask, movers, counts, planes, halo_c, halo_x, movers, counts)
-
-
-def migrate_kernel(doms, message, out, landed, ssem, rsem):
+    )(nbr, mask, movers, counts, planes, *[pltpu.with_memory_space_constraint(t, pltpu.VMEM) for t in tables])
+
+
+def migrate_kernel(message, out, first, landed, ssem, rsem):
     grp, me = lax.axis_index("grp"), lax.axis_index("dom")
+    y, z, core = me // 16, lax.rem(me // 2, 8), lax.rem(me, 2)
+    place = y * 2 + core
+
+    def across(k):
+        other = lax.rem(place + k, 8)
+        return other // 2, z, lax.rem(other, 2)
+
+    def along(k):
+        return y, lax.rem(z + k, 8), core
+
+    def device(at):
+        return (grp, at[0] * 16 + at[1] * 2 + at[2])
+
     barrier = pltpu.get_barrier_semaphore()
-
-    def greet(k, carry):
-        other = lax.rem(me + k, doms)
-        pl.semaphore_signal(barrier, inc=1, device_id=(grp, other), device_id_type=MESH)
-        return carry
-
-    lax.fori_loop(1, doms, greet, 0)
-    landed[me] = message[me]
-    pl.semaphore_wait(barrier, doms - 1)
-
-    def copy(k):
-        other = lax.rem(me + k, doms)
+    for k in range(1, 8):
+        for at in (across(k), along(k)):
+            pl.semaphore_signal(barrier, inc=1, device_id=device(at), device_id_type=MESH)
+    first[y, core] = message[y, :, core]
+    pl.semaphore_wait(barrier, 14)
+
+    def hop_one(k):
+        at = across(k)
         return pltpu.make_async_remote_copy(
-            src_ref=message.at[other],
-            dst_ref=landed.at[me],
-            send_sem=ssem.at[k],
-            recv_sem=rsem.at[k],
-            device_id=(grp, other),
+            src_ref=message.at[at[0], :, at[2]],
+            dst_ref=first.at[y, core],
+            send_sem=ssem.at[0, k],
+            recv_sem=rsem.at[0, k],
+            device_id=device(at),
             device_id_type=MESH,
         )
 
-    def send(k, carry):
-        copy(k).start()
-        return carry
-
-    def finish(k, carry):
-        copy(k).wait()
-        return carry
-
-    lax.fori_loop(1, doms, send, 0)
-    lax.fori_loop(1, doms, finish, 0)
-    for g in range(doms // 8):
-        cols = slice(g * 128, g * 128 + 128)
+    def hop_two(k):
+        at = along(k)
+        return pltpu.make_async_remote_copy(
+            src_ref=first.at[:, :, at[1]],
+            dst_ref=landed.at[:, z],
+            send_sem=ssem.at[1, k],
+            recv_sem=rsem.at[1, k],
+            device_id=device(at),
+            device_id_type=MESH,
+        )
+
+    one, two = [hop_one(k) for k in range(1, 8)], [hop_two(k) for k in range(1, 8)]
+    for copy in one:
+        copy.start()
+    for copy in one:
+        copy.wait_recv()
+    for copy in two:
+        copy.start()
+    landed[:, z] = first[:, :, z]
+    for copy in one:
+        copy.wait_send()
+    for copy in two:
+        copy.wait()
+    for g in range(8):
         for h in range(2):
+            v = landed[g // 2, pl.ds((g % 2) * 4, 4), :, h, :].reshape(8, 128)
             rows = 8 if h == 0 else 4
-            v = swap_groups(landed[pl.ds(g * 8, 8), h, :])
-            out[8 * h : 8 * h + rows, cols] = v[:rows]
+            out[8 * h : 8 * h + rows, g * 128 : g * 128 + 128] = swap_groups(v)[:rows]
 
 
 def migrate(message):
-    doms = message.shape[0]
     vmem = pl.BlockSpec(memory_space=pltpu.VMEM)
     return pl.pallas_call(
-        functools.partial(migrate_kernel, doms),
-        out_shape=jax.ShapeDtypeStruct((12, doms * 16), F32),
+        migrate_kernel,
+        out_shape=jax.ShapeDtypeStruct((12, 1024), F32),
         in_specs=[vmem],
         out_specs=vmem,
         scratch_shapes=[
-            pltpu.VMEM((doms, 2, 128), F32),
-            pltpu.SemaphoreType.DMA((doms,)),
-            pltpu.SemaphoreType.DMA((doms,)),
+            pltpu.VMEM((4, 2, 8, 2, 128), F32),
+            pltpu.VMEM((4, 8, 2, 2, 128), F32),
+            pltpu.SemaphoreType.DMA((2, 8)),
+            pltpu.SemaphoreType.DMA((2, 8)),
         ],
-        compiler_params=pltpu.CompilerParams(collective_id=1, has_side_effects=True),
-    )(message)
+        compiler_params=pltpu.CompilerParams(
+            collective_id=1, has_side_effects=True, vmem_limit_bytes=VMEM_LIMIT
+        ),
+    )(pltpu.with_memory_space_constraint(message, pltpu.VMEM))
 
 
 def on_device(state, neighbours, pair_mask, send_lists, send_counts, movers, mover_counts):
-    planes = state.transpose(1, 0, 2)
-    halo_c, halo_x = exchange(send_lists[0], send_counts, planes)
-    kept, message = local_step(
-        neighbours.T, pair_mask.T, movers[0].T, planes, halo_c, halo_x.reshape(3, 4 * HB, 128), mover_counts
-    )
-    arrivals = migrate(message.reshape(-1, 2, 128))
+    def far(x):
+        return pltpu.with_memory_space_constraint(x, pltpu.HBM)
+
+    planes = pltpu.with_memory_space_constraint(state.transpose(1, 0, 2), pltpu.VMEM)
+    slots, counts = far(movers[0].T), far(mover_counts)
+    tables = exchange(far(send_lists[0]), far(send_counts), planes, slots, counts)
+    kept, message = local_step(far(neighbours.T), far(pair_mask.T), slots, counts, planes, tables)
+    arrivals = migrate(message.reshape(4, 8, 2, 2, 128))
     return kept.transpose(1, 0, 2), arrivals
 
 

time: 77.8 us -> 72.2 us (0.928)
  Pallas kernels: 75.5 us -> 69.3 us
    pallas_call x1, Pallas kernels: 42.2 us -> 38.9 us  [local_step(): pl.pallas_call(local_kernel, out_shape=(jax.ShapeDtypeStruct((12, NB, 128...]
    pallas_call x2, Pallas kernels: 33.3 us -> 30.5 us  [the longest x1 16 us: migrate(): pl.pallas_call(migrate_kernel, out_shape=jax.ShapeDtypeStruct((12, 1024),...]
    unnamed x1 -> x3, local copies, waits for them, and re-layouts: 1.47 us -> 2.03 us
where the time goes in v2:
time: 72.2 us; the launch traced here: 72 us
  Pallas kernels  69.3 us (96%)
  local copies, waits for them, and re-layouts  2.03 us (3%)
    pallas_call x1, Pallas kernels, local_step(): pl.pallas_call(local_kernel, out_shape=(jax.ShapeDtypeStruct((12, NB, 128...  38.9 us
    pallas_call x1, Pallas kernels, migrate(): pl.pallas_call(migrate_kernel, out_shape=jax.ShapeDtypeStruct((12, 1024),...  16 us
    pallas_call x1, Pallas kernels, exchange(): pl.pallas_call(exchange_kernel, out_shape=(pltpu.VMEM((3, 4 * HB, 128), F...  14.4 us
    unnamed x3, local copies, waits for them, and re-layouts  2.03 us

profile of v2, /device:TPU:1, one launch (start us, length us, event | category | flops | bytes accessed | tf_op | source)
XLA Modules:
  0.0 72.0 jit_solution(15460497589964007894)
XLA Ops:
  0.6 0.0 copy-start
  0.6 1.4 %copy-done = f32[256,12,128]{2,0,1:T(8,128)S(1)} copy-done((f32[256,12,128]{2,0,1:T(8,128)S(1)}, f32[256,12,128]{2,0,1:T(8,128)}, u32[]{:S(2)}) %copy-start) | copy-done | bytes 1572888
  2.0 14.4 %shard_map.86 = (f32[3,256,128]{2,1,0:T(8,128)S(1)}, bf16[513,48,128]{2,1,0:T(8,128)(2,1)S(1)}, bf16[256,48,128]{2,1,0:T(8,128)(2,1)S(1)}, bf16[513,32,128]{2,1,0:T(8,128)(2,1)S(1)}, f32[256,128]{1,0:T(8,128)S(1)}) custom-call(s32[4,64]{1,0:T(4,128)} %bitcast.16, s32[1,4]{1,0:T(1,128)} %counts.1, f32[12,256,128]{2,1,0:T(8,128)S(1)} %bitcast.9, ...), custom_call_target="tpu_custom_call" | custom-call | tf_op jit(solution)/shard_map/pallas_call | solution.py:187
  16.5 38.9 %shard_map.87 = (f32[12,256,128]{2,1,0:T(8,128)}, f32[128,128]{1,0:T(8,128)S(1)}) custom-call(s32[4,256]{1,0:T(4,128)} %bitcast.14, s32[4,256]{1,0:T(4,128)} %bitcast.15, s32[16,64]{1,0:T(8,128)} %bitcast.13, s32[1,64]{1,0:T(1,128)} %counts_s.1, f32[12,256,128]{2,1,0:T(8,128)S(1)} %bitcast.10, f32[3,256,128]{2,1,0:T(8,128)S(1)} %get-tuple-element.9.halo_x, ...), custom_call_target="tpu_custom_call" | custom-call | tf_op jit(solution)/shard_map/pallas_call | solution.py:365
  55.3 16.0 %shard_map.88 = f32[12,1024]{1,0:T(8,128)S(1)} custom-call(f32[4,8,2,2,128]{4,3,2,1,0:T(2,128)S(1)} %bitcast.11), custom_call_target="tpu_custom_call" | custom-call | tf_op jit(solution)/shard_map/pallas_call | solution.py:449
  71.4 0.6 copy.10
Async XLA Ops:
  0.6 1.4 %copy-start = (f32[256,12,128]{2,0,1:T(8,128)S(1)}, f32[256,12,128]{2,0,1:T(8,128)}, u32[]{:S(2)}) copy-start(f32[256,12,128]{2,0,1:T(8,128)} %param.7) | copy-start | bytes 4718596

commit v3 on v2

--- a/solution.py
+++ b/solution.py
@@ -13,7 +13,8 @@
 NC = 512
 FR = 48
 CR = 32
-U = 8
+U = 32
+RING = 8
 REACH = 2.0
 NT = (((1,), (1,)), ((), ()))
 TN = (((0,), (0,)), ((), ()))
@@ -115,7 +116,7 @@
 
     centre = [0.5 * jnp.max(st[c]) + 0.5 * jnp.min(st[c]) for c in range(3)]
 
-    def features(source, own):
+    def features(source, own, first, last):
         def body(q, carry):
             rows = pl.ds(pl.multiple_of(q * 32, 32), 32)
             zero, one = jnp.zeros((32, 128), F32), jnp.ones((32, 128), F32)
@@ -131,9 +132,9 @@
                     tab_p[pl.ds(q * 256 + c, 32, stride=8), :] = plane
             return carry
 
-        lax.fori_loop(0, NB // 32, body, 0)
-
-    def convert(own):
+        lax.fori_loop(first // 32, last // 32, body, 0)
+
+    def convert(own, first, last):
         def body(q, carry):
             for u in range(8):
                 b = q * 8 + u
@@ -148,10 +149,10 @@
                     own_feat[b] = jnp.concatenate([p1, p1, p1, p2, p2, p3], 0).astype(BF16)
             return carry
 
-        lax.fori_loop(0, NB // 8, body, 0)
-
-    features(st, True)
-    convert(True)
+        lax.fori_loop(first // 8, last // 8, body, 0)
+
+    features(st, True, 0, NB)
+    convert(True, 0, NB)
     feat[NC] = jnp.zeros((FR, 128), BF16)
     car[NC] = jnp.zeros((CR, 128), BF16)
 
@@ -173,13 +174,18 @@
 
         @pl.when(has[p])
         def _(p=p):
+            for copy in copies(p ^ 1):
+                copy.wait_recv()
+
+        features(halo_x, False, p * HB, p * HB + HB)
+        convert(False, p * HB, p * HB + HB)
+
+    for p in range(4):
+
+        @pl.when(has[p])
+        def _(p=p):
             for copy in copies(p):
                 copy.wait_send()
-            for copy in copies(p ^ 1):
-                copy.wait_recv()
-
-    features(halo_x, False)
-    convert(False)
 
 
 def exchange(lists, counts, planes, movers, mover_counts):
@@ -225,10 +231,10 @@
 
 
 def local_kernel(
-    nbr, mask, movers_s, counts_s, st, halo_x, feat, own_feat, car, stay_ref, kept, message,
-    tab_x, sums, upd, *stages,
+    nbr, mask, movers_s, counts_s, st, halo_x, feat, own_feat, car, stay_ref, kept_out, message,
+    tab_x, sums, upd, kept, *stages,
 ):
-    dist, high, low = stages[:U], stages[U : 2 * U], stages[2 * U :]
+    dist, parts = stages[:RING], stages[RING:-1]
     wide = None
     for c in range(3):
         half = 0.5 * jnp.max(st[c]) - 0.5 * jnp.min(st[c])
@@ -257,29 +263,28 @@
             cols = slice(half * 256, half * 256 + 256)
             s = jnp.maximum(dist[u][:, cols], 0.0)
             h, rest = split(s * s * s)
-            high[u][:, cols] = h
-            low[u][:, cols] = rest
+            parts[u][0:128, cols] = h
+            parts[u][128:256, cols] = rest
 
     def contract(i, u):
         c = jnp.concatenate([car[slot(k, i)] for k in range(4)], 1)
-        r = lax.dot_general(c, high[u][...], NT, preferred_element_type=F32)
-        r = r + lax.dot_general(c, low[u][...], NT, preferred_element_type=F32)
-        store_sums(i, r)
+        r = lax.dot_general(c, parts[u][...], NT, preferred_element_type=F32)
+        store_sums(i, r[:, 0:128] + r[:, 128:256])
 
     @pl.when(close)
     def _():
         def body(t, carry):
             for u in range(U):
                 i = t * U + u
-                contract(jnp.maximum(i - 2, 0), (u - 2) % U)
-                weigh((u - 1) % U)
-                measure(i, u)
+                contract(jnp.maximum(i - 2, 0), (u - 2) % RING)
+                weigh((u - 1) % RING)
+                measure(i, u % RING)
             return carry
 
         lax.fori_loop(0, NB // U, body, 0)
-        contract(NB - 2, U - 2)
-        weigh(U - 1)
-        contract(NB - 1, U - 1)
+        contract(NB - 2, RING - 2)
+        weigh(RING - 1)
+        contract(NB - 1, RING - 1)
 
     @pl.when(jnp.logical_not(close))
     def _():
@@ -341,22 +346,26 @@
 
     lax.fori_loop(0, NB // 32, advance, 0)
 
-    upd[pl.ds(NB * 16, 16), :] = jnp.zeros((16, 128), F32)
+    out_copy = pltpu.make_async_copy(kept, kept_out, stages[-1])
+    out_copy.start()
     lane = lax.broadcasted_iota(jnp.int32, (16, 128), 1)
 
     def gather(g, carry):
+        count = jnp.zeros((16, 128), jnp.int32)
+        for q in range(8):
+            count = jnp.where(lax.shift_right_logical(lane, 4) == q, counts_s[0, g * 8 + q], count)
         acc = jnp.zeros((16, 128), F32)
         for t in range(128):
             m = movers_s[t % 16, g * 8 + t // 16]
-            b, ln = lax.shift_right_logical(m, 7), m & 127
-            b = jnp.where(t % 16 < counts_s[0, g * 8 + t // 16], b, NB)
-            v = upd[pl.ds(pl.multiple_of(b * 16, 16), 16), :]
-            acc = jnp.where(lane == t, pltpu.roll(v, (t - ln) & 127, 1), acc)
+            at = pl.multiple_of(lax.shift_right_logical(m, 7) * 16, 16)
+            acc = jnp.where(lane == t, pltpu.roll(upd[pl.ds(at, 16), :], (t - m) & 127, 1), acc)
+        acc = jnp.where((lane & 15) < count, acc, 0.0)
         for h in range(2):
             message[pl.ds(g * 16 + h, 8, stride=2), :] = swap_groups(acc[8 * h : 8 * h + 8])
         return carry
 
     lax.fori_loop(0, movers_s.shape[1] // 8, gather, 0)
+    out_copy.wait()
 
 
 def local_step(nbr, mask, movers, counts, planes, tables):
@@ -365,17 +374,19 @@
     return pl.pallas_call(
         local_kernel,
         out_shape=(
-            jax.ShapeDtypeStruct((12, NB, 128), F32),
+            pltpu.HBM((12, NB, 128), F32),
             pltpu.VMEM((2 * doms, 128), F32),
         ),
         in_specs=[smem] * 4 + [vmem] * 6,
-        out_specs=(vmem, vmem),
+        out_specs=(pl.BlockSpec(memory_space=pl.ANY), vmem),
         scratch_shapes=[
             pltpu.VMEM((NC * 8, 128), F32),
             pltpu.VMEM((NB * 8, 128), F32),
-            pltpu.VMEM((NB * 16 + 16, 128), F32),
-            *[pltpu.VMEM((128, 512), F32)] * U,
-            *[pltpu.VMEM((128, 512), BF16)] * (2 * U),
+            pltpu.VMEM((NB * 16, 128), F32),
+            pltpu.VMEM((12, NB, 128), F32),
+            *[pltpu.VMEM((128, 512), F32)] * RING,
+            *[pltpu.VMEM((256, 512), BF16)] * RING,
+            pltpu.SemaphoreType.DMA,
         ],
         compiler_params=pltpu.CompilerParams(vmem_limit_bytes=VMEM_LIMIT),
     )(nbr, mask, movers, counts, planes, *[pltpu.with_memory_space_constraint(t, pltpu.VMEM) for t in tables])

time: 72.2 us -> 64.3 us (0.89)
  Pallas kernels: 69.3 us -> 61.4 us
    pallas_call x1, Pallas kernels: 38.9 us -> 31.4 us  [local_step(): pl.pallas_call(local_kernel, out_shape=(pltpu.HBM((12, NB, 128), F32), pl...]
    pallas_call x1, Pallas kernels: 14.4 us -> 13.7 us  [exchange(): pl.pallas_call(exchange_kernel, out_shape=(pltpu.VMEM((3, 4 * HB, 128), F...]
where the time goes in v3:
time: 64.3 us; the launch traced here: 64.1 us
  Pallas kernels  61.4 us (95%)
  local copies, waits for them, and re-layouts  2.03 us (3%)
  between operations  0.66 us (1%)
    pallas_call x1, Pallas kernels, local_step(): pl.pallas_call(local_kernel, out_shape=(pltpu.HBM((12, NB, 128), F32), pl...  31.4 us
    pallas_call x1, Pallas kernels, migrate(): pl.pallas_call(migrate_kernel, out_shape=jax.ShapeDtypeStruct((12, 1024),...  16.3 us
    pallas_call x1, Pallas kernels, exchange(): pl.pallas_call(exchange_kernel, out_shape=(pltpu.VMEM((3, 4 * HB, 128), F...  13.7 us
    unnamed x3, local copies, waits for them, and re-layouts  2.03 us

profile of v3, /device:TPU:1, one launch (start us, length us, event | category | flops | bytes accessed | tf_op | source)
XLA Modules:
  0.0 64.1 jit_solution(16470759146375826142)
XLA Ops:
  0.6 0.0 copy-start
  0.6 1.4 %copy-done = f32[256,12,128]{2,0,1:T(8,128)S(1)} copy-done((f32[256,12,128]{2,0,1:T(8,128)S(1)}, f32[256,12,128]{2,0,1:T(8,128)}, u32[]{:S(2)}) %copy-start) | copy-done | bytes 1572888
  2.0 13.7 %shard_map.86 = (f32[3,256,128]{2,1,0:T(8,128)S(1)}, bf16[513,48,128]{2,1,0:T(8,128)(2,1)S(1)}, bf16[256,48,128]{2,1,0:T(8,128)(2,1)S(1)}, bf16[513,32,128]{2,1,0:T(8,128)(2,1)S(1)}, f32[256,128]{1,0:T(8,128)S(1)}) custom-call(s32[4,64]{1,0:T(4,128)} %bitcast.16, s32[1,4]{1,0:T(1,128)} %counts.1, f32[12,256,128]{2,1,0:T(8,128)S(1)} %bitcast.9, ...), custom_call_target="tpu_custom_call" | custom-call | tf_op jit(solution)/shard_map/pallas_call | solution.py:193
  15.7 31.4 %shard_map.87 = (f32[12,256,128]{2,1,0:T(8,128)}, f32[128,128]{1,0:T(8,128)S(1)}) custom-call(s32[4,256]{1,0:T(4,128)} %bitcast.14, s32[4,256]{1,0:T(4,128)} %bitcast.15, s32[16,64]{1,0:T(8,128)} %bitcast.13, s32[1,64]{1,0:T(1,128)} %counts_s.1, f32[12,256,128]{2,1,0:T(8,128)S(1)} %bitcast.10, f32[3,256,128]{2,1,0:T(8,128)S(1)} %get-tuple-element.9.halo_x, ...), custom_call_target="tpu_custom_call" | custom-call | tf_op jit(solution)/shard_map/pallas_call | solution.py:374
  47.1 16.3 %shard_map.88 = f32[12,1024]{1,0:T(8,128)S(1)} custom-call(f32[4,8,2,2,128]{4,3,2,1,0:T(2,128)S(1)} %bitcast.11), custom_call_target="tpu_custom_call" | custom-call | tf_op jit(solution)/shard_map/pallas_call | solution.py:460
  63.5 0.6 copy.10
Async XLA Ops:
  0.6 1.4 %copy-start = (f32[256,12,128]{2,0,1:T(8,128)S(1)}, f32[256,12,128]{2,0,1:T(8,128)}, u32[]{:S(2)}) copy-start(f32[256,12,128]{2,0,1:T(8,128)} %param.7) | copy-start | bytes 4718596

commit v4 on v3

--- a/solution.py
+++ b/solution.py
@@ -14,7 +14,8 @@
 FR = 48
 CR = 32
 U = 32
-RING = 8
+UA = 8
+RB = 4
 REACH = 2.0
 NT = (((1,), (1,)), ((), ()))
 TN = (((0,), (0,)), ((), ()))
@@ -30,6 +31,33 @@
     return out
 
 
+def split(w):
+    h = w.astype(BF16)
+    return h, (w - h.astype(F32)).astype(BF16)
+
+
+def weights(dist, lane, row, parts, out_row):
+    s = jnp.maximum(dist[row : row + 128, lane : lane + 128], 0.0)
+    h, rest = split(s * s * s)
+    parts[out_row : out_row + 128, 0:128] = h
+    parts[out_row : out_row + 128, 128:256] = rest
+
+
+def beside(one, two):
+    return jnp.concatenate(
+        [
+            jnp.concatenate([one, jnp.zeros_like(two)], 1),
+            jnp.concatenate([jnp.zeros_like(one), two], 1),
+        ],
+        0,
+    )
+
+
+def fold(r):
+    r = r[:, 0:128] + r[:, 128:256]
+    return r[0:8] + r[8:16] + r[16:24]
+
+
 def pieces(v):
     first = v.astype(BF16).astype(F32)
     rest = v - first
@@ -37,9 +65,25 @@
     return first, second, rest - second
 
 
+def order_slots(nbr, mask):
+    a, b, c, d = (jnp.where(mask[k : k + 1, :] == 0, NC, nbr[k : k + 1, :]) for k in range(4))
+    which = jnp.full_like(a, 4)
+    for k, slots in ((3, d), (2, c), (1, b), (0, a)):
+        which = jnp.where((slots < NB) | (slots == NC), k, which)
+    first = jnp.where(which == 0, a, jnp.where(which == 1, b, jnp.where(which == 2, c, d)))
+    rows = [
+        jnp.where(which == 4, NC, first),
+        jnp.where(which == 0, b, a),
+        jnp.where(which <= 1, c, b),
+        jnp.where(which <= 2, d, c),
+        jnp.where(which == 4, d, NC),
+    ]
+    return jnp.concatenate(rows + [jnp.full_like(a, NC)] * 3, 0)
+
+
 def exchange_kernel(
-    lists, counts, st, movers, mover_counts, halo_x, feat, own_feat, car, stay,
-    halo_c, tab_c, tab_x, near_x, tab_p, send_c, pick_x, send_x, ssem, rsem,
+    lists, counts, st, movers, mover_counts, nbr, mask, halo_x, feat, own_feat, car, stay, near_sums, order_out,
+    halo_c, tab_c, tab_x, near_x, tab_p, send_c, pick_x, send_x, ssem, rsem, order, order_sem, *stages,
 ):
     grp, dom = lax.axis_index("grp"), lax.axis_index("dom")
     n_grp, n_dom = lax.axis_size("grp"), lax.axis_size("dom")
@@ -151,6 +195,9 @@
 
         lax.fori_loop(first // 8, last // 8, body, 0)
 
+    order_out[...] = order_slots(nbr, mask)
+    order_copy = pltpu.make_async_copy(order_out, order, order_sem)
+    order_copy.start()
     features(st, True, 0, NB)
     convert(True, 0, NB)
     feat[NC] = jnp.zeros((FR, 128), BF16)
@@ -170,6 +217,47 @@
         gone = gone + lax.dot_general(in_block, in_lane, NT, preferred_element_type=F32)
     stay[...] = 1.0 - gone
 
+    dist, parts = stages[:RB], stages[RB:]
+
+    def measure(p, u):
+        one, two = 2 * p, 2 * p + 1
+        near = jnp.concatenate([feat[order[0, one]], feat[order[0, two]]], 0)
+        dist[u][...] = lax.dot_general(
+            near, beside(own_feat[one], own_feat[two]), TN, preferred_element_type=F32
+        )
+
+    def weigh(u):
+        for n in range(2):
+            weights(dist[u], n * 128, 0, parts[u], n * 128)
+
+    def contract(p, u):
+        c = beside(car[order[0, 2 * p]], car[order[0, 2 * p + 1]])
+        r = jnp.dot(c, parts[u][...], preferred_element_type=F32)
+        at = pl.multiple_of(p * 16, 16)
+        near_sums[pl.ds(at, 8), :] = fold(r[0:CR])
+        near_sums[pl.ds(at + 8, 8), :] = fold(r[CR:])
+
+    order_copy.wait()
+    measure(0, 0)
+    weigh(0)
+    measure(1, 1)
+
+    def steps(t, last):
+        for u in range(UA):
+            p = t * UA + u
+            contract(p, u % RB)
+            if not last or u < UA - 1:
+                weigh((u + 1) % RB)
+            if not last or u < UA - 2:
+                measure(p + 2, (u + 2) % RB)
+
+    def body(t, carry):
+        steps(t, False)
+        return carry
+
+    lax.fori_loop(0, NB // 2 // UA - 1, body, 0)
+    steps(NB // 2 // UA - 1, True)
+
     for p in range(4):
 
         @pl.when(has[p])
@@ -188,7 +276,7 @@
                 copy.wait_send()
 
 
-def exchange(lists, counts, planes, movers, mover_counts):
+def exchange(lists, counts, planes, movers, mover_counts, nbr, mask):
     smem, vmem = pl.BlockSpec(memory_space=pltpu.SMEM), pl.BlockSpec(memory_space=pltpu.VMEM)
     return pl.pallas_call(
         exchange_kernel,
@@ -198,9 +286,11 @@
             pltpu.VMEM((NB, FR, 128), BF16),
             pltpu.VMEM((NC + 1, CR, 128), BF16),
             pltpu.VMEM((NB, 128), F32),
+            pltpu.VMEM((NB * 8, 128), F32),
+            pltpu.VMEM((8, NB), jnp.int32),
         ),
-        in_specs=[smem, smem, vmem, vmem, vmem],
-        out_specs=(vmem,) * 5,
+        in_specs=[smem, smem] + [vmem] * 5,
+        out_specs=(vmem,) * 7,
         scratch_shapes=[
             pltpu.VMEM((4 * HB * 8, 128), F32),
             pltpu.VMEM((NB, 8, 128), F32),
@@ -212,11 +302,15 @@
             pltpu.VMEM((3, 4, HB, 128), F32),
             pltpu.SemaphoreType.DMA((4, 2)),
             pltpu.SemaphoreType.DMA((4, 2)),
+            pltpu.SMEM((8, NB), jnp.int32),
+            pltpu.SemaphoreType.DMA,
+            *[pltpu.VMEM((128, 256), F32)] * RB,
+            *[pltpu.VMEM((256, 256), BF16)] * RB,
         ],
         compiler_params=pltpu.CompilerParams(
             collective_id=0, has_side_effects=True, vmem_limit_bytes=VMEM_LIMIT
         ),
-    )(lists, counts, planes, movers, mover_counts)
+    )(lists, counts, planes, movers, mover_counts, nbr, mask)
 
 
 def swap_groups(v):
@@ -231,60 +325,84 @@
 
 
 def local_kernel(
-    nbr, mask, movers_s, counts_s, st, halo_x, feat, own_feat, car, stay_ref, kept_out, message,
-    tab_x, sums, upd, kept, *stages,
+    order, nbr, mask, movers_s, counts_s, st, halo_x, feat, own_feat, car, stay_ref, near_sums, kept_out, message,
+    tab_x, sums, upd, kept, late, *stages,
 ):
-    dist, parts = stages[:RING], stages[RING:-1]
+    dist, parts = stages[:RB], stages[RB:-1]
     wide = None
     for c in range(3):
         half = 0.5 * jnp.max(st[c]) - 0.5 * jnp.min(st[c])
         wide = half if wide is None else jnp.maximum(wide, half)
     close = wide <= REACH
 
-    def slot(k, i):
-        return jnp.where(mask[k, i] == 0, NC, nbr[k, i])
-
-    def store_sums(i, r):
-        sums[pl.ds(pl.multiple_of(i * 8, 8), 8), :] = r[0:8] + r[8:16] + r[16:24]
-
-    def split(w):
-        h = w.astype(BF16)
-        return h, (w - h.astype(F32)).astype(BF16)
-
-    def measure(i, u):
-        for half in range(2):
-            near = jnp.concatenate([feat[slot(2 * half + k, i)] for k in range(2)], 1)
-            dist[u][:, half * 256 : half * 256 + 256] = lax.dot_general(
-                own_feat[i], near, TN, preferred_element_type=F32
+    def measure(p, u):
+        one, two = 2 * p, 2 * p + 1
+        mine = beside(own_feat[one], own_feat[two])
+        for k in range(3):
+            near = jnp.concatenate([feat[order[k + 1, one]], feat[order[k + 1, two]]], 0)
+            dist[u][k * 128 : k * 128 + 128, :] = lax.dot_general(
+                near, mine, TN, preferred_element_type=F32
             )
 
     def weigh(u):
-        for half in range(2):
-            cols = slice(half * 256, half * 256 + 256)
-            s = jnp.maximum(dist[u][:, cols], 0.0)
-            h, rest = split(s * s * s)
-            parts[u][0:128, cols] = h
-            parts[u][128:256, cols] = rest
-
-    def contract(i, u):
-        c = jnp.concatenate([car[slot(k, i)] for k in range(4)], 1)
-        r = lax.dot_general(c, parts[u][...], NT, preferred_element_type=F32)
-        store_sums(i, r[:, 0:128] + r[:, 128:256])
+        for n in range(2):
+            for k in range(3):
+                weights(dist[u], n * 128, k * 128, parts[u], (n * 3 + k) * 128)
+
+    def contract(p, u):
+        c = beside(*[
+            jnp.concatenate([car[order[k, i]] for k in (1, 2, 3)], 1) for i in (2 * p, 2 * p + 1)
+        ])
+        r = jnp.dot(c, parts[u][...], preferred_element_type=F32)
+        at = pl.multiple_of(p * 16, 16)
+        sums[pl.ds(at, 8), :] = fold(r[0:CR])
+        sums[pl.ds(at + 8, 8), :] = fold(r[CR:])
 
     @pl.when(close)
     def _():
-        def body(t, carry):
+        def body(t, n_late):
             for u in range(U):
-                i = t * U + u
-                contract(jnp.maximum(i - 2, 0), (u - 2) % RING)
-                weigh((u - 1) % RING)
-                measure(i, u % RING)
+                p = t * U + u
+                for i in (2 * p, 2 * p + 1):
+                    late[n_late] = i
+                    n_late = n_late + jnp.where(order[4, i] == NC, 0, 1)
+                contract(jnp.maximum(p - 2, 0), (u - 2) % RB)
+                weigh((u - 1) % RB)
+                measure(p, u % RB)
+            return n_late
+
+        n_late = lax.fori_loop(0, NB // 2 // U, body, 0)
+        contract(NB // 2 - 2, RB - 2)
+        weigh(RB - 1)
+        contract(NB // 2 - 1, RB - 1)
+
+        def rest(t, carry):
+            blocks, slots = [], []
+            for u in range(2 * RB):
+                on = t * 2 * RB + u < n_late
+                blocks.append(jnp.where(on, late[t * 2 * RB + u], 0))
+                slots.append(jnp.where(on, order[4, blocks[u]], NC))
+                lanes = slice((u % 2) * 128, (u % 2) * 128 + 128)
+                dist[u // 2][0:128, lanes] = lax.dot_general(
+                    feat[slots[u]], own_feat[blocks[u]], TN, preferred_element_type=F32
+                )
+            for u in range(2 * RB):
+                weights(dist[u // 2], (u % 2) * 128, 0, parts[u // 2], (u % 2) * 128)
+            for u in range(2 * RB):
+                rows = slice((u % 2) * 128, (u % 2) * 128 + 128)
+                r = jnp.dot(car[slots[u]], parts[u // 2][rows, :], preferred_element_type=F32)
+                at = pl.ds(pl.multiple_of(blocks[u] * 8, 8), 8)
+                sums[at, :] = sums[at, :] + fold(r)
             return carry
 
-        lax.fori_loop(0, NB // U, body, 0)
-        contract(NB - 2, RING - 2)
-        weigh(RING - 1)
-        contract(NB - 1, RING - 1)
+        lax.fori_loop(0, (n_late + 2 * RB - 1) // (2 * RB), rest, 0)
+
+        def add(q, carry):
+            at = pl.ds(pl.multiple_of(q * 256, 256), 256)
+            sums[at, :] = sums[at, :] + near_sums[at, :]
+            return carry
+
+        lax.fori_loop(0, NB // 32, add, 0)
 
     @pl.when(jnp.logical_not(close))
     def _():
@@ -308,11 +426,11 @@
                     s = s - delta * delta
                 s = jnp.maximum(s, 0.0)
                 h, rest = split(s * s * s)
-                cc = car[slot(k, i)]
-                r = lax.dot_general(cc, h, NT, preferred_element_type=F32)
-                return total + r + lax.dot_general(cc, rest, NT, preferred_element_type=F32)
-
-            store_sums(i, lax.fori_loop(0, 4, pair, jnp.zeros((CR, 128), F32)))
+                cc = car[jnp.where(mask[k, i] == 0, NC, nbr[k, i])]
+                return total + lax.dot_general(cc, jnp.concatenate([h, rest], 0), NT, preferred_element_type=F32)
+
+            total = lax.fori_loop(0, 4, pair, jnp.zeros((CR, 256), F32))
+            sums[pl.ds(pl.multiple_of(i * 8, 8), 8), :] = fold(total)
             return carry
 
         lax.fori_loop(0, NB, body, 0)
@@ -368,7 +486,7 @@
     out_copy.wait()
 
 
-def local_step(nbr, mask, movers, counts, planes, tables):
+def local_step(order, nbr, mask, movers, counts, planes, tables):
     smem, vmem = pl.BlockSpec(memory_space=pltpu.SMEM), pl.BlockSpec(memory_space=pltpu.VMEM)
     doms = movers.shape[1]
     return pl.pallas_call(
@@ -377,19 +495,20 @@
             pltpu.HBM((12, NB, 128), F32),
             pltpu.VMEM((2 * doms, 128), F32),
         ),
-        in_specs=[smem] * 4 + [vmem] * 6,
+        in_specs=[smem] * 5 + [vmem] * 7,
         out_specs=(pl.BlockSpec(memory_space=pl.ANY), vmem),
         scratch_shapes=[
             pltpu.VMEM((NC * 8, 128), F32),
             pltpu.VMEM((NB * 8, 128), F32),
             pltpu.VMEM((NB * 16, 128), F32),
             pltpu.VMEM((12, NB, 128), F32),
-            *[pltpu.VMEM((128, 512), F32)] * RING,
-            *[pltpu.VMEM((256, 512), BF16)] * RING,
+            pltpu.SMEM((NB + 4 * RB,), jnp.int32),
+            *[pltpu.VMEM((384, 256), F32)] * RB,
+            *[pltpu.VMEM((768, 256), BF16)] * RB,
             pltpu.SemaphoreType.DMA,
         ],
         compiler_params=pltpu.CompilerParams(vmem_limit_bytes=VMEM_LIMIT),
-    )(nbr, mask, movers, counts, planes, *[pltpu.with_memory_space_constraint(t, pltpu.VMEM) for t in tables])
+    )(pltpu.with_memory_space_constraint(order, pltpu.VMEM), nbr, mask, movers, counts, planes, *[pltpu.with_memory_space_constraint(t, pltpu.VMEM) for t in tables])
 
 
 def migrate_kernel(message, out, first, landed, ssem, rsem):
@@ -480,8 +599,9 @@
 
     planes = pltpu.with_memory_space_constraint(state.transpose(1, 0, 2), pltpu.VMEM)
     slots, counts = far(movers[0].T), far(mover_counts)
-    tables = exchange(far(send_lists[0]), far(send_counts), planes, slots, counts)
-    kept, message = local_step(far(neighbours.T), far(pair_mask.T), slots, counts, planes, tables)
+    nbr, mask = far(neighbours.T), far(pair_mask.T)
+    *tables, order = exchange(far(send_lists[0]), far(send_counts), planes, slots, counts, nbr, mask)
+    kept, message = local_step(order, nbr, mask, slots, counts, planes, tables)
     arrivals = migrate(message.reshape(4, 8, 2, 2, 128))
     return kept.transpose(1, 0, 2), arrivals
 

time: 64.3 us -> 61.5 us (0.956)
  Pallas kernels: 61.4 us -> 58.5 us
    pallas_call x1, Pallas kernels: 31.4 us -> 22.7 us  [local_step(): pl.pallas_call(local_kernel, out_shape=(pltpu.HBM((12, NB, 128), F32), pl...]
    pallas_call x1, Pallas kernels: 13.7 us -> 18.6 us  [exchange(): pl.pallas_call(exchange_kernel, out_shape=(pltpu.VMEM((3, 4 * HB, 128), F...]
    pallas_call x1, Pallas kernels: 16.3 us -> 17.3 us  [migrate(): pl.pallas_call(migrate_kernel, out_shape=jax.ShapeDtypeStruct((12, 1024),...]
where the time goes in v4:
time: 61.5 us; the launch traced here: 61.2 us
  Pallas kernels  58.5 us (95%)
  local copies, waits for them, and re-layouts  2.03 us (3%)
  between operations  0.66 us (1%)
    pallas_call x1, Pallas kernels, local_step(): pl.pallas_call(local_kernel, out_shape=(pltpu.HBM((12, NB, 128), F32), pl...  22.7 us
    pallas_call x1, Pallas kernels, exchange(): pl.pallas_call(exchange_kernel, out_shape=(pltpu.VMEM((3, 4 * HB, 128), F...  18.6 us
    pallas_call x1, Pallas kernels, migrate(): pl.pallas_call(migrate_kernel, out_shape=jax.ShapeDtypeStruct((12, 1024),...  17.3 us
    unnamed x3, local copies, waits for them, and re-layouts  2.03 us

profile of v4, /device:TPU:1, one launch (start us, length us, event | category | flops | bytes accessed | tf_op | source)
XLA Modules:
  0.0 61.2 jit_solution(8183422470306617423)
XLA Ops:
  0.6 0.0 copy-start
  0.6 1.4 %copy-done = f32[256,12,128]{2,0,1:T(8,128)S(1)} copy-done((f32[256,12,128]{2,0,1:T(8,128)S(1)}, f32[256,12,128]{2,0,1:T(8,128)}, u32[]{:S(2)}) %copy-start) | copy-done | bytes 1572888
  2.0 18.6 %shard_map.86 = (f32[3,256,128]{2,1,0:T(8,128)S(1)}, bf16[513,48,128]{2,1,0:T(8,128)(2,1)S(1)}, bf16[256,48,128]{2,1,0:T(8,128)(2,1)S(1)}, bf16[513,32,128]{2,1,...) custom-call(s32[4,64]{1,0:T(4,128)} %bitcast.18, s32[1,4]{1,0:T(1,128)} %counts.1, ...), custom_call_target="tpu_custom_call" | custom-call | tf_op jit(solution)/shard_map/pallas_call | solution.py:281
  20.6 22.7 %shard_map.87 = (f32[12,256,128]{2,1,0:T(8,128)}, f32[128,128]{1,0:T(8,128)S(1)}) custom-call(s32[8,256]{1,0:T(8,128)S(1)} %get-tuple-element.11.order, s32[4,256]{1,0:T(4,128)} %bitcast.15, s32[4,256]{1,0:T(4,128)} %bitcast.17, s32[16,64]{1,0:T(8,128)} %bitcast.13, s32[1,64]{1,0:T(1,128)} %counts_s.1, f32[12,256,128]{2,1,0:T(8,128)S(1)} %bitcast.10, ...), custom_call_target="tpu_custom_call" | custom-call | tf_op jit(solution)/shard_map/pallas_call | solution.py:492
  43.3 17.3 %shard_map.88 = f32[12,1024]{1,0:T(8,128)S(1)} custom-call(f32[4,8,2,2,128]{4,3,2,1,0:T(2,128)S(1)} %bitcast.11), custom_call_target="tpu_custom_call" | custom-call | tf_op jit(solution)/shard_map/pallas_call | solution.py:579
  60.6 0.6 %copy.10 = f32[12,1024]{1,0:T(8,128)} copy(f32[12,1024]{1,0:T(8,128)S(1)} %shard_map.88) | data formatting | bytes 98304
Async XLA Ops:
  0.6 1.4 %copy-start = (f32[256,12,128]{2,0,1:T(8,128)S(1)}, f32[256,12,128]{2,0,1:T(8,128)}, u32[]{:S(2)}) copy-start(f32[256,12,128]{2,0,1:T(8,128)} %param.7) | copy-start | bytes 4718596

commit v5 on v3

--- a/solution.py
+++ b/solution.py
@@ -14,7 +14,8 @@
 FR = 48
 CR = 32
 U = 32
-RING = 8
+RB = 4
+LOADS = 4
 REACH = 2.0
 NT = (((1,), (1,)), ((), ()))
 TN = (((0,), (0,)), ((), ()))
@@ -30,6 +31,33 @@
     return out
 
 
+def split(w):
+    h = w.astype(BF16)
+    return h, (w - h.astype(F32)).astype(BF16)
+
+
+def weights(dist, lane, row, parts, out_row):
+    s = jnp.maximum(dist[row : row + 128, lane : lane + 128], 0.0)
+    h, rest = split(s * s * s)
+    parts[out_row : out_row + 128, 0:128] = h
+    parts[out_row : out_row + 128, 128:256] = rest
+
+
+def beside(one, two):
+    return jnp.concatenate(
+        [
+            jnp.concatenate([one, jnp.zeros_like(two)], 1),
+            jnp.concatenate([jnp.zeros_like(one), two], 1),
+        ],
+        0,
+    )
+
+
+def fold(r):
+    r = r[:, 0:128] + r[:, 128:256]
+    return r[0:8] + r[8:16] + r[16:24]
+
+
 def pieces(v):
     first = v.astype(BF16).astype(F32)
     rest = v - first
@@ -38,13 +66,22 @@
 
 
 def exchange_kernel(
-    lists, counts, st, movers, mover_counts, halo_x, feat, own_feat, car, stay,
-    halo_c, tab_c, tab_x, near_x, tab_p, send_c, pick_x, send_x, ssem, rsem,
+    lists, counts, state, movers, mover_counts, halo_x, feat, own_feat, car, stay, st,
+    halo_c, tab_c, tab_x, near_x, tab_p, send_c, pick_x, send_x, ssem, rsem, load_sem,
 ):
     grp, dom = lax.axis_index("grp"), lax.axis_index("dom")
     n_grp, n_dom = lax.axis_size("grp"), lax.axis_size("dom")
     has = [dom > 0, dom < n_dom - 1, grp > 0, grp < n_grp - 1]
     peer = [(grp, dom - 1), (grp, dom + 1), (grp - 1, dom), (grp + 1, dom)]
+    chunk = NB // LOADS
+    loads = [
+        pltpu.make_async_copy(
+            state.at[:, pl.ds(q * chunk, chunk)], st.at[:, pl.ds(q * chunk, chunk)], load_sem.at[q]
+        )
+        for q in range(LOADS)
+    ]
+    for load in loads:
+        load.start()
     barrier = pltpu.get_barrier_semaphore()
     for p in range(4):
 
@@ -60,7 +97,9 @@
             tab_x[rows, c, :] = st[c, rows, :]
         return carry
 
-    lax.fori_loop(0, NB // 32, build, 0)
+    for q, load in enumerate(loads):
+        load.wait()
+        lax.fori_loop(q * chunk // 32, (q + 1) * chunk // 32, build, 0)
 
     def copies(p):
         slot = p ^ 1
@@ -198,9 +237,10 @@
             pltpu.VMEM((NB, FR, 128), BF16),
             pltpu.VMEM((NC + 1, CR, 128), BF16),
             pltpu.VMEM((NB, 128), F32),
+            pltpu.VMEM((12, NB, 128), F32),
         ),
-        in_specs=[smem, smem, vmem, vmem, vmem],
-        out_specs=(vmem,) * 5,
+        in_specs=[smem, smem, pl.BlockSpec(memory_space=pl.ANY), vmem, vmem],
+        out_specs=(vmem,) * 6,
         scratch_shapes=[
             pltpu.VMEM((4 * HB * 8, 128), F32),
             pltpu.VMEM((NB, 8, 128), F32),
@@ -212,6 +252,7 @@
             pltpu.VMEM((3, 4, HB, 128), F32),
             pltpu.SemaphoreType.DMA((4, 2)),
             pltpu.SemaphoreType.DMA((4, 2)),
+            pltpu.SemaphoreType.DMA((LOADS,)),
         ],
         compiler_params=pltpu.CompilerParams(
             collective_id=0, has_side_effects=True, vmem_limit_bytes=VMEM_LIMIT
@@ -234,7 +275,7 @@
     nbr, mask, movers_s, counts_s, st, halo_x, feat, own_feat, car, stay_ref, kept_out, message,
     tab_x, sums, upd, kept, *stages,
 ):
-    dist, parts = stages[:RING], stages[RING:-1]
+    dist, parts = stages[:RB], stages[RB:-1]
     wide = None
     for c in range(3):
         half = 0.5 * jnp.max(st[c]) - 0.5 * jnp.min(st[c])
@@ -244,47 +285,43 @@
     def slot(k, i):
         return jnp.where(mask[k, i] == 0, NC, nbr[k, i])
 
-    def store_sums(i, r):
-        sums[pl.ds(pl.multiple_of(i * 8, 8), 8), :] = r[0:8] + r[8:16] + r[16:24]
-
-    def split(w):
-        h = w.astype(BF16)
-        return h, (w - h.astype(F32)).astype(BF16)
-
-    def measure(i, u):
-        for half in range(2):
-            near = jnp.concatenate([feat[slot(2 * half + k, i)] for k in range(2)], 1)
-            dist[u][:, half * 256 : half * 256 + 256] = lax.dot_general(
-                own_feat[i], near, TN, preferred_element_type=F32
+    def measure(p, u):
+        one, two = 2 * p, 2 * p + 1
+        mine = beside(own_feat[one], own_feat[two])
+        for k in range(4):
+            near = jnp.concatenate([feat[slot(k, one)], feat[slot(k, two)]], 0)
+            dist[u][k * 128 : k * 128 + 128, :] = lax.dot_general(
+                near, mine, TN, preferred_element_type=F32
             )
 
     def weigh(u):
-        for half in range(2):
-            cols = slice(half * 256, half * 256 + 256)
-            s = jnp.maximum(dist[u][:, cols], 0.0)
-            h, rest = split(s * s * s)
-            parts[u][0:128, cols] = h
-            parts[u][128:256, cols] = rest
-
-    def contract(i, u):
-        c = jnp.concatenate([car[slot(k, i)] for k in range(4)], 1)
-        r = lax.dot_general(c, parts[u][...], NT, preferred_element_type=F32)
-        store_sums(i, r[:, 0:128] + r[:, 128:256])
+        for n in range(2):
+            for k in range(4):
+                weights(dist[u], n * 128, k * 128, parts[u], (n * 4 + k) * 128)
+
+    def contract(p, u):
+        c = beside(*[
+            jnp.concatenate([car[slot(k, i)] for k in range(4)], 1) for i in (2 * p, 2 * p + 1)
+        ])
+        r = jnp.dot(c, parts[u][...], preferred_element_type=F32)
+        at = pl.multiple_of(p * 16, 16)
+        sums[pl.ds(at, 8), :] = fold(r[0:CR])
+        sums[pl.ds(at + 8, 8), :] = fold(r[CR:])
 
     @pl.when(close)
     def _():
         def body(t, carry):
             for u in range(U):
-                i = t * U + u
-                contract(jnp.maximum(i - 2, 0), (u - 2) % RING)
-                weigh((u - 1) % RING)
-                measure(i, u % RING)
+                p = t * U + u
+                contract(jnp.maximum(p - 2, 0), (u - 2) % RB)
+                weigh((u - 1) % RB)
+                measure(p, u % RB)
             return carry
 
-        lax.fori_loop(0, NB // U, body, 0)
-        contract(NB - 2, RING - 2)
-        weigh(RING - 1)
-        contract(NB - 1, RING - 1)
+        lax.fori_loop(0, NB // 2 // U, body, 0)
+        contract(NB // 2 - 2, RB - 2)
+        weigh(RB - 1)
+        contract(NB // 2 - 1, RB - 1)
 
     @pl.when(jnp.logical_not(close))
     def _():
@@ -309,10 +346,10 @@
                 s = jnp.maximum(s, 0.0)
                 h, rest = split(s * s * s)
                 cc = car[slot(k, i)]
-                r = lax.dot_general(cc, h, NT, preferred_element_type=F32)
-                return total + r + lax.dot_general(cc, rest, NT, preferred_element_type=F32)
-
-            store_sums(i, lax.fori_loop(0, 4, pair, jnp.zeros((CR, 128), F32)))
+                return total + lax.dot_general(cc, jnp.concatenate([h, rest], 0), NT, preferred_element_type=F32)
+
+            total = lax.fori_loop(0, 4, pair, jnp.zeros((CR, 256), F32))
+            sums[pl.ds(pl.multiple_of(i * 8, 8), 8), :] = fold(total)
             return carry
 
         lax.fori_loop(0, NB, body, 0)
@@ -351,12 +388,15 @@
     lane = lax.broadcasted_iota(jnp.int32, (16, 128), 1)
 
     def gather(g, carry):
+        def to(z):
+            return (g // 2) * 16 + 2 * z + g % 2
+
         count = jnp.zeros((16, 128), jnp.int32)
         for q in range(8):
-            count = jnp.where(lax.shift_right_logical(lane, 4) == q, counts_s[0, g * 8 + q], count)
+            count = jnp.where(lax.shift_right_logical(lane, 4) == q, counts_s[0, to(q)], count)
         acc = jnp.zeros((16, 128), F32)
         for t in range(128):
-            m = movers_s[t % 16, g * 8 + t // 16]
+            m = movers_s[t % 16, to(t // 16)]
             at = pl.multiple_of(lax.shift_right_logical(m, 7) * 16, 16)
             acc = jnp.where(lane == t, pltpu.roll(upd[pl.ds(at, 16), :], (t - m) & 127, 1), acc)
         acc = jnp.where((lane & 15) < count, acc, 0.0)
@@ -384,12 +424,12 @@
             pltpu.VMEM((NB * 8, 128), F32),
             pltpu.VMEM((NB * 16, 128), F32),
             pltpu.VMEM((12, NB, 128), F32),
-            *[pltpu.VMEM((128, 512), F32)] * RING,
-            *[pltpu.VMEM((256, 512), BF16)] * RING,
+            *[pltpu.VMEM((512, 256), F32)] * RB,
+            *[pltpu.VMEM((1024, 256), BF16)] * RB,
             pltpu.SemaphoreType.DMA,
         ],
         compiler_params=pltpu.CompilerParams(vmem_limit_bytes=VMEM_LIMIT),
-    )(nbr, mask, movers, counts, planes, *[pltpu.with_memory_space_constraint(t, pltpu.VMEM) for t in tables])
+    )(nbr, mask, movers, counts, pltpu.with_memory_space_constraint(planes, pltpu.VMEM), *[pltpu.with_memory_space_constraint(t, pltpu.VMEM) for t in tables])
 
 
 def migrate_kernel(message, out, first, landed, ssem, rsem):
@@ -411,14 +451,14 @@
     for k in range(1, 8):
         for at in (across(k), along(k)):
             pl.semaphore_signal(barrier, inc=1, device_id=device(at), device_id_type=MESH)
-    first[y, core] = message[y, :, core]
+    first[place] = message[place]
     pl.semaphore_wait(barrier, 14)
 
     def hop_one(k):
         at = across(k)
         return pltpu.make_async_remote_copy(
-            src_ref=message.at[at[0], :, at[2]],
-            dst_ref=first.at[y, core],
+            src_ref=message.at[at[0] * 2 + at[2]],
+            dst_ref=first.at[place],
             send_sem=ssem.at[0, k],
             recv_sem=rsem.at[0, k],
             device_id=device(at),
@@ -428,8 +468,8 @@
     def hop_two(k):
         at = along(k)
         return pltpu.make_async_remote_copy(
-            src_ref=first.at[:, :, at[1]],
-            dst_ref=landed.at[:, z],
+            src_ref=first.at[:, at[1]],
+            dst_ref=landed.at[z],
             send_sem=ssem.at[1, k],
             recv_sem=rsem.at[1, k],
             device_id=device(at),
@@ -443,14 +483,14 @@
         copy.wait_recv()
     for copy in two:
         copy.start()
-    landed[:, z] = first[:, :, z]
+    landed[z] = first[:, z]
     for copy in one:
         copy.wait_send()
     for copy in two:
         copy.wait()
     for g in range(8):
         for h in range(2):
-            v = landed[g // 2, pl.ds((g % 2) * 4, 4), :, h, :].reshape(8, 128)
+            v = landed[pl.ds((g % 2) * 4, 4), pl.ds((g // 2) * 2, 2), h, :].reshape(8, 128)
             rows = 8 if h == 0 else 4
             out[8 * h : 8 * h + rows, g * 128 : g * 128 + 128] = swap_groups(v)[:rows]
 
@@ -463,8 +503,8 @@
         in_specs=[vmem],
         out_specs=vmem,
         scratch_shapes=[
-            pltpu.VMEM((4, 2, 8, 2, 128), F32),
-            pltpu.VMEM((4, 8, 2, 2, 128), F32),
+            pltpu.VMEM((8, 8, 2, 128), F32),
+            pltpu.VMEM((8, 8, 2, 128), F32),
             pltpu.SemaphoreType.DMA((2, 8)),
             pltpu.SemaphoreType.DMA((2, 8)),
         ],
@@ -478,11 +518,11 @@
     def far(x):
         return pltpu.with_memory_space_constraint(x, pltpu.HBM)
 
-    planes = pltpu.with_memory_space_constraint(state.transpose(1, 0, 2), pltpu.VMEM)
+    planes = far(state.transpose(1, 0, 2))
     slots, counts = far(movers[0].T), far(mover_counts)
-    tables = exchange(far(send_lists[0]), far(send_counts), planes, slots, counts)
+    *tables, planes = exchange(far(send_lists[0]), far(send_counts), planes, slots, counts)
     kept, message = local_step(far(neighbours.T), far(pair_mask.T), slots, counts, planes, tables)
-    arrivals = migrate(message.reshape(4, 8, 2, 2, 128))
+    arrivals = migrate(message.reshape(8, 8, 2, 128))
     return kept.transpose(1, 0, 2), arrivals
 
 

time: 64.3 us -> 60.3 us (0.938)
  Pallas kernels: 61.4 us -> 58.8 us
  local copies, waits for them, and re-layouts: 2.03 us -> 0.63 us
    pallas_call x1, Pallas kernels: 31.4 us -> 27.7 us  [local_step(): pl.pallas_call(local_kernel, out_shape=(pltpu.HBM((12, NB, 128), F32), pl...]
    unnamed x3 -> x1, local copies, waits for them, and re-layouts: 2.03 us -> 0.63 us
    pallas_call x1, Pallas kernels: 16.3 us -> 17.2 us  [migrate(): pl.pallas_call(migrate_kernel, out_shape=jax.ShapeDtypeStruct((12, 1024),...]
where the time goes in v5:
time: 60.3 us; the launch traced here: 60.1 us
  Pallas kernels  58.8 us (98%)
  between operations  0.65 us (1%)
  local copies, waits for them, and re-layouts  0.63 us (1%)
    pallas_call x1, Pallas kernels, local_step(): pl.pallas_call(local_kernel, out_shape=(pltpu.HBM((12, NB, 128), F32), pl...  27.7 us
    pallas_call x1, Pallas kernels, migrate(): pl.pallas_call(migrate_kernel, out_shape=jax.ShapeDtypeStruct((12, 1024),...  17.2 us
    pallas_call x1, Pallas kernels, exchange(): pl.pallas_call(exchange_kernel, out_shape=(pltpu.VMEM((3, 4 * HB, 128), F...  13.9 us

profile of v5, /device:TPU:1, one launch (start us, length us, event | category | flops | bytes accessed | tf_op | source)
XLA Modules:
  0.0 60.1 jit_solution(8038773289043664351)
XLA Ops:
  0.6 13.9 %shard_map.86 = (f32[3,256,128]{2,1,0:T(8,128)S(1)}, bf16[513,48,128]{2,1,0:T(8,128)(2,1)S(1)}, bf16[256,48,128]{2,1,0:T(8,128)(2,1)S(1)}, bf16[513,32,128]{2,1,...) custom-call(s32[4,64]{1,0:T(4,128)} %bitcast.15, s32[1,4]{1,0:T(1,128)} %counts.1, ...), custom_call_target="tpu_custom_call" | custom-call | tf_op jit(solution)/shard_map/pallas_call | solution.py:232
  14.5 27.7 %shard_map.87 = (f32[12,256,128]{2,1,0:T(8,128)}, f32[128,128]{1,0:T(8,128)S(1)}) custom-call(s32[4,256]{1,0:T(4,128)} %bitcast.13, s32[4,256]{1,0:T(4,128)} %bitcast.14, s32[16,64]{1,0:T(8,128)} %bitcast.12, s32[1,64]{1,0:T(1,128)} %counts_s.1, f32[12,256,128]{2,1,0:T(8,128)S(1)} %get-tuple-element.10.st, f32[3,256,128]{2,1,0:T(8,128)S(1)} %get-tuple-element.11.halo_x, ...), custom_call_target="tpu_custom_call" | custom-call | tf_op jit(solution)/shard_map/pallas_call | solution.py:414
  42.2 17.2 %shard_map.88 = f32[12,1024]{1,0:T(8,128)S(1)} custom-call(f32[8,8,2,128]{3,2,1,0:T(2,128)S(1)} %bitcast.9), custom_call_target="tpu_custom_call" | custom-call | tf_op jit(solution)/shard_map/pallas_call | solution.py:500
  59.4 0.6 %copy.10 = f32[12,1024]{1,0:T(8,128)} copy(f32[12,1024]{1,0:T(8,128)S(1)} %shard_map.88) | data formatting | bytes 98304

commit v6 on v5

--- a/solution.py
+++ b/solution.py
@@ -272,10 +272,10 @@
 
 
 def local_kernel(
-    nbr, mask, movers_s, counts_s, st, halo_x, feat, own_feat, car, stay_ref, kept_out, message,
-    tab_x, sums, upd, kept, *stages,
+    nbr, mask, st, halo_x, feat, own_feat, car, stay_ref, kept_out, upd,
+    tab_x, sums, kept, out_sem, *stages,
 ):
-    dist, parts = stages[:RB], stages[RB:-1]
+    dist, parts = stages[:RB], stages[RB:]
     wide = None
     for c in range(3):
         half = 0.5 * jnp.max(st[c]) - 0.5 * jnp.min(st[c])
@@ -375,16 +375,64 @@
         stay = stay_ref[rows, :]
         for c, plane in enumerate(updated):
             kept[c, rows, :] = plane * stay
-            upd[pl.ds(q * 512 + c, 32, stride=16), :] = plane
+            upd[rows, c, :] = plane
         zero = jnp.zeros((32, 128), F32)
         for c in range(12, 16):
-            upd[pl.ds(q * 512 + c, 32, stride=16), :] = zero
+            upd[rows, c, :] = zero
+        leave(q).start()
         return carry
 
+    def leave(q):
+        rows = pl.ds(pl.multiple_of(q * 32, 32), 32)
+        return pltpu.make_async_copy(kept.at[:, rows], kept_out.at[:, rows], out_sem.at[q])
+
     lax.fori_loop(0, NB // 32, advance, 0)
-
-    out_copy = pltpu.make_async_copy(kept, kept_out, stages[-1])
-    out_copy.start()
+    for q in range(NB // 32):
+        leave(q).wait()
+
+
+def local_step(nbr, mask, planes, tables):
+    smem, vmem = pl.BlockSpec(memory_space=pltpu.SMEM), pl.BlockSpec(memory_space=pltpu.VMEM)
+    return pl.pallas_call(
+        local_kernel,
+        out_shape=(
+            pltpu.HBM((12, NB, 128), F32),
+            pltpu.VMEM((NB, 16, 128), F32),
+        ),
+        in_specs=[smem] * 2 + [vmem] * 6,
+        out_specs=(pl.BlockSpec(memory_space=pl.ANY), vmem),
+        scratch_shapes=[
+            pltpu.VMEM((NC * 8, 128), F32),
+            pltpu.VMEM((NB * 8, 128), F32),
+            pltpu.VMEM((12, NB, 128), F32),
+            pltpu.SemaphoreType.DMA((NB // 32,)),
+            *[pltpu.VMEM((512, 256), F32)] * RB,
+            *[pltpu.VMEM((1024, 256), BF16)] * RB,
+        ],
+        compiler_params=pltpu.CompilerParams(vmem_limit_bytes=VMEM_LIMIT),
+    )(nbr, mask, pltpu.with_memory_space_constraint(planes, pltpu.VMEM), *[pltpu.with_memory_space_constraint(t, pltpu.VMEM) for t in tables])
+
+
+def migrate_kernel(movers_s, counts_s, upd, out, message, first, landed, ssem, rsem):
+    grp, me = lax.axis_index("grp"), lax.axis_index("dom")
+    y, z, core = me // 16, lax.rem(me // 2, 8), lax.rem(me, 2)
+    place = y * 2 + core
+
+    def across(k):
+        other = lax.rem(place + k, 8)
+        return other // 2, z, lax.rem(other, 2)
+
+    def along(k):
+        return y, lax.rem(z + k, 8), core
+
+    def device(at):
+        return (grp, at[0] * 16 + at[1] * 2 + at[2])
+
+    barrier = pltpu.get_barrier_semaphore()
+    for k in range(1, 8):
+        for at in (across(k), along(k)):
+            pl.semaphore_signal(barrier, inc=1, device_id=device(at), device_id_type=MESH)
+
     lane = lax.broadcasted_iota(jnp.int32, (16, 128), 1)
 
     def gather(g, carry):
@@ -397,60 +445,13 @@
         acc = jnp.zeros((16, 128), F32)
         for t in range(128):
             m = movers_s[t % 16, to(t // 16)]
-            at = pl.multiple_of(lax.shift_right_logical(m, 7) * 16, 16)
-            acc = jnp.where(lane == t, pltpu.roll(upd[pl.ds(at, 16), :], (t - m) & 127, 1), acc)
+            acc = jnp.where(lane == t, pltpu.roll(upd[lax.shift_right_logical(m, 7)], (t - m) & 127, 1), acc)
         acc = jnp.where((lane & 15) < count, acc, 0.0)
         for h in range(2):
-            message[pl.ds(g * 16 + h, 8, stride=2), :] = swap_groups(acc[8 * h : 8 * h + 8])
+            message[g, :, h, :] = swap_groups(acc[8 * h : 8 * h + 8])
         return carry
 
-    lax.fori_loop(0, movers_s.shape[1] // 8, gather, 0)
-    out_copy.wait()
-
-
-def local_step(nbr, mask, movers, counts, planes, tables):
-    smem, vmem = pl.BlockSpec(memory_space=pltpu.SMEM), pl.BlockSpec(memory_space=pltpu.VMEM)
-    doms = movers.shape[1]
-    return pl.pallas_call(
-        local_kernel,
-        out_shape=(
-            pltpu.HBM((12, NB, 128), F32),
-            pltpu.VMEM((2 * doms, 128), F32),
-        ),
-        in_specs=[smem] * 4 + [vmem] * 6,
-        out_specs=(pl.BlockSpec(memory_space=pl.ANY), vmem),
-        scratch_shapes=[
-            pltpu.VMEM((NC * 8, 128), F32),
-            pltpu.VMEM((NB * 8, 128), F32),
-            pltpu.VMEM((NB * 16, 128), F32),
-            pltpu.VMEM((12, NB, 128), F32),
-            *[pltpu.VMEM((512, 256), F32)] * RB,
-            *[pltpu.VMEM((1024, 256), BF16)] * RB,
-            pltpu.SemaphoreType.DMA,
-        ],
-        compiler_params=pltpu.CompilerParams(vmem_limit_bytes=VMEM_LIMIT),
-    )(nbr, mask, movers, counts, pltpu.with_memory_space_constraint(planes, pltpu.VMEM), *[pltpu.with_memory_space_constraint(t, pltpu.VMEM) for t in tables])
-
-
-def migrate_kernel(message, out, first, landed, ssem, rsem):
-    grp, me = lax.axis_index("grp"), lax.axis_index("dom")
-    y, z, core = me // 16, lax.rem(me // 2, 8), lax.rem(me, 2)
-    place = y * 2 + core
-
-    def across(k):
-        other = lax.rem(place + k, 8)
-        return other // 2, z, lax.rem(other, 2)
-
-    def along(k):
-        return y, lax.rem(z + k, 8), core
-
-    def device(at):
-        return (grp, at[0] * 16 + at[1] * 2 + at[2])
-
-    barrier = pltpu.get_barrier_semaphore()
-    for k in range(1, 8):
-        for at in (across(k), along(k)):
-            pl.semaphore_signal(barrier, inc=1, device_id=device(at), device_id_type=MESH)
+    lax.fori_loop(0, 8, gather, 0)
     first[place] = message[place]
     pl.semaphore_wait(barrier, 14)
 
@@ -495,14 +496,15 @@
             out[8 * h : 8 * h + rows, g * 128 : g * 128 + 128] = swap_groups(v)[:rows]
 
 
-def migrate(message):
-    vmem = pl.BlockSpec(memory_space=pltpu.VMEM)
+def migrate(movers, counts, upd):
+    smem, vmem = pl.BlockSpec(memory_space=pltpu.SMEM), pl.BlockSpec(memory_space=pltpu.VMEM)
     return pl.pallas_call(
         migrate_kernel,
         out_shape=jax.ShapeDtypeStruct((12, 1024), F32),
-        in_specs=[vmem],
+        in_specs=[smem, smem, vmem],
         out_specs=vmem,
         scratch_shapes=[
+            pltpu.VMEM((8, 8, 2, 128), F32),
             pltpu.VMEM((8, 8, 2, 128), F32),
             pltpu.VMEM((8, 8, 2, 128), F32),
             pltpu.SemaphoreType.DMA((2, 8)),
@@ -511,7 +513,7 @@
         compiler_params=pltpu.CompilerParams(
             collective_id=1, has_side_effects=True, vmem_limit_bytes=VMEM_LIMIT
         ),
-    )(pltpu.with_memory_space_constraint(message, pltpu.VMEM))
+    )(movers, counts, pltpu.with_memory_space_constraint(upd, pltpu.VMEM))
 
 
 def on_device(state, neighbours, pair_mask, send_lists, send_counts, movers, mover_counts):
@@ -521,8 +523,8 @@
     planes = far(state.transpose(1, 0, 2))
     slots, counts = far(movers[0].T), far(mover_counts)
     *tables, planes = exchange(far(send_lists[0]), far(send_counts), planes, slots, counts)
-    kept, message = local_step(far(neighbours.T), far(pair_mask.T), slots, counts, planes, tables)
-    arrivals = migrate(message.reshape(8, 8, 2, 128))
+    kept, upd = local_step(far(neighbours.T), far(pair_mask.T), planes, tables)
+    arrivals = migrate(slots, counts, upd)
     return kept.transpose(1, 0, 2), arrivals
 
 

time: 60.3 us -> 59.9 us (level)
    pallas_call x1, Pallas kernels: 27.7 us -> 25.3 us  [local_step(): pl.pallas_call(local_kernel, out_shape=(pltpu.HBM((12, NB, 128), F32), pl...]
    pallas_call x1, Pallas kernels: 17.2 us -> 19.3 us  [migrate(): pl.pallas_call(migrate_kernel, out_shape=jax.ShapeDtypeStruct((12, 1024),...]
where the time goes in v6:
time: 59.9 us; the launch traced here: 59.7 us
  Pallas kernels  58.4 us (97%)
  between operations  0.65 us (1%)
  local copies, waits for them, and re-layouts  0.63 us (1%)
    pallas_call x1, Pallas kernels, local_step(): pl.pallas_call(local_kernel, out_shape=(pltpu.HBM((12, NB, 128), F32), pl...  25.3 us
    pallas_call x1, Pallas kernels, migrate(): pl.pallas_call(migrate_kernel, out_shape=jax.ShapeDtypeStruct((12, 1024),...  19.3 us
    pallas_call x1, Pallas kernels, exchange(): pl.pallas_call(exchange_kernel, out_shape=(pltpu.VMEM((3, 4 * HB, 128), F...  13.9 us

profile of v6, /device:TPU:1, one launch (start us, length us, event | category | flops | bytes accessed | tf_op | source)
XLA Modules:
  0.0 59.7 jit_solution(15496255258809142194)
XLA Ops:
  0.6 13.9 %shard_map.86 = (f32[3,256,128]{2,1,0:T(8,128)S(1)}, bf16[513,48,128]{2,1,0:T(8,128)(2,1)S(1)}, bf16[256,48,128]{2,1,0:T(8,128)(2,1)S(1)}, bf16[513,32,128]{2,1,...) custom-call(s32[4,64]{1,0:T(4,128)} %bitcast.13, s32[1,4]{1,0:T(1,128)} %counts.1, ...), custom_call_target="tpu_custom_call" | custom-call | tf_op jit(solution)/shard_map/pallas_call | solution.py:232
  14.5 25.3 %shard_map.87 = (f32[12,256,128]{2,1,0:T(8,128)}, f32[256,16,128]{2,1,0:T(8,128)S(1)}) custom-call(s32[4,256]{1,0:T(4,128)} %bitcast.11, s32[4,256]{1,0:T(4,128)} %bitcast.12, f32[12,256,128]{2,1,0:T(8,128)S(1)} %get-tuple-element.10.st, f32[3,256,128]{2,1,0:T(8,128)S(1)} %get-tuple-element.11.halo_x, bf16[513,48,128]{2,1,0:T(8,128)(2,1)S(1)} %get-tuple-element.12.feat, ...), custom_call_target="tpu_custom_call" | custom-call | tf_op jit(solution)/shard_map/pallas_call | solution.py:396
  39.8 19.3 %shard_map.88 = f32[12,1024]{1,0:T(8,128)S(1)} custom-call(s32[16,64]{1,0:T(8,128)} %bitcast.10, s32[1,64]{1,0:T(1,128)} %counts_s.1, f32[256,16,128]{2,1,0:T(8,128)S(1)} %get-tuple-element.17.upd), custom_call_target="tpu_custom_call" | custom-call | tf_op jit(solution)/shard_map/pallas_call | solution.py:501
  59.1 0.6 %copy.10 = f32[12,1024]{1,0:T(8,128)} copy(f32[12,1024]{1,0:T(8,128)S(1)} %shard_map.88) | data formatting | bytes 98304

commit v7 on v6

--- a/solution.py
+++ b/solution.py
@@ -13,7 +13,7 @@
 NC = 512
 FR = 48
 CR = 32
-U = 32
+U = 64
 RB = 4
 LOADS = 4
 REACH = 2.0
@@ -413,87 +413,58 @@
     )(nbr, mask, pltpu.with_memory_space_constraint(planes, pltpu.VMEM), *[pltpu.with_memory_space_constraint(t, pltpu.VMEM) for t in tables])
 
 
-def migrate_kernel(movers_s, counts_s, upd, out, message, first, landed, ssem, rsem):
+def migrate_kernel(movers_s, counts_s, upd, out, message, landed, ssem, rsem):
     grp, me = lax.axis_index("grp"), lax.axis_index("dom")
-    y, z, core = me // 16, lax.rem(me // 2, 8), lax.rem(me, 2)
-    place = y * 2 + core
-
-    def across(k):
-        other = lax.rem(place + k, 8)
-        return other // 2, z, lax.rem(other, 2)
-
-    def along(k):
-        return y, lax.rem(z + k, 8), core
-
-    def device(at):
-        return (grp, at[0] * 16 + at[1] * 2 + at[2])
+    doms = 64
+
+    def device(k):
+        return (grp, lax.rem(me + k, doms))
 
     barrier = pltpu.get_barrier_semaphore()
-    for k in range(1, 8):
-        for at in (across(k), along(k)):
-            pl.semaphore_signal(barrier, inc=1, device_id=device(at), device_id_type=MESH)
+    for k in range(1, doms):
+        pl.semaphore_signal(barrier, inc=1, device_id=device(k), device_id_type=MESH)
 
     lane = lax.broadcasted_iota(jnp.int32, (16, 128), 1)
 
     def gather(g, carry):
-        def to(z):
-            return (g // 2) * 16 + 2 * z + g % 2
-
         count = jnp.zeros((16, 128), jnp.int32)
         for q in range(8):
-            count = jnp.where(lax.shift_right_logical(lane, 4) == q, counts_s[0, to(q)], count)
+            count = jnp.where(lax.shift_right_logical(lane, 4) == q, counts_s[0, g * 8 + q], count)
         acc = jnp.zeros((16, 128), F32)
         for t in range(128):
-            m = movers_s[t % 16, to(t // 16)]
+            m = movers_s[t % 16, g * 8 + t // 16]
             acc = jnp.where(lane == t, pltpu.roll(upd[lax.shift_right_logical(m, 7)], (t - m) & 127, 1), acc)
         acc = jnp.where((lane & 15) < count, acc, 0.0)
         for h in range(2):
-            message[g, :, h, :] = swap_groups(acc[8 * h : 8 * h + 8])
+            message[pl.ds(g * 8, 8), h, :] = swap_groups(acc[8 * h : 8 * h + 8])
         return carry
 
     lax.fori_loop(0, 8, gather, 0)
-    first[place] = message[place]
-    pl.semaphore_wait(barrier, 14)
-
-    def hop_one(k):
-        at = across(k)
+    landed[me] = message[me]
+    pl.semaphore_wait(barrier, doms - 1)
+
+    def copy(k):
         return pltpu.make_async_remote_copy(
-            src_ref=message.at[at[0] * 2 + at[2]],
-            dst_ref=first.at[place],
-            send_sem=ssem.at[0, k],
-            recv_sem=rsem.at[0, k],
-            device_id=device(at),
+            src_ref=message.at[lax.rem(me + k, doms)],
+            dst_ref=landed.at[me],
+            send_sem=ssem.at[k],
+            recv_sem=rsem.at[k],
+            device_id=device(k),
             device_id_type=MESH,
         )
 
-    def hop_two(k):
-        at = along(k)
-        return pltpu.make_async_remote_copy(
-            src_ref=first.at[:, at[1]],
-            dst_ref=landed.at[z],
-            send_sem=ssem.at[1, k],
-            recv_sem=rsem.at[1, k],
-            device_id=device(at),
-            device_id_type=MESH,
-        )
-
-    one, two = [hop_one(k) for k in range(1, 8)], [hop_two(k) for k in range(1, 8)]
-    for copy in one:
-        copy.start()
-    for copy in one:
-        copy.wait_recv()
-    for copy in two:
-        copy.start()
-    landed[z] = first[:, z]
-    for copy in one:
-        copy.wait_send()
-    for copy in two:
-        copy.wait()
-    for g in range(8):
+    copies = [copy(k) for k in range(1, doms)]
+    for c in copies:
+        c.start()
+    for c in copies:
+        c.wait_recv()
+    for g in range(doms // 8):
         for h in range(2):
-            v = landed[pl.ds((g % 2) * 4, 4), pl.ds((g // 2) * 2, 2), h, :].reshape(8, 128)
             rows = 8 if h == 0 else 4
-            out[8 * h : 8 * h + rows, g * 128 : g * 128 + 128] = swap_groups(v)[:rows]
+            v = swap_groups(landed[pl.ds(g * 8, 8), h, :])
+            out[8 * h : 8 * h + rows, g * 128 : g * 128 + 128] = v[:rows]
+    for c in copies:
+        c.wait_send()
 
 
 def migrate(movers, counts, upd):
@@ -504,11 +475,10 @@
         in_specs=[smem, smem, vmem],
         out_specs=vmem,
         scratch_shapes=[
-            pltpu.VMEM((8, 8, 2, 128), F32),
-            pltpu.VMEM((8, 8, 2, 128), F32),
-            pltpu.VMEM((8, 8, 2, 128), F32),
-            pltpu.SemaphoreType.DMA((2, 8)),
-            pltpu.SemaphoreType.DMA((2, 8)),
+            pltpu.VMEM((64, 2, 128), F32),
+            pltpu.VMEM((64, 2, 128), F32),
+            pltpu.SemaphoreType.DMA((64,)),
+            pltpu.SemaphoreType.DMA((64,)),
         ],
         compiler_params=pltpu.CompilerParams(
             collective_id=1, has_side_effects=True, vmem_limit_bytes=VMEM_LIMIT

time: 59.9 us -> 59.2 us (0.988)
  Pallas kernels: 58.4 us -> 57.7 us
where the time goes in v7:
time: 59.2 us; the launch traced here: 59 us
  Pallas kernels  57.7 us (97%)
  between operations  0.65 us (1%)
  local copies, waits for them, and re-layouts  0.63 us (1%)
    pallas_call x1, Pallas kernels, local_step(): pl.pallas_call(local_kernel, out_shape=(pltpu.HBM((12, NB, 128), F32), pl...  24.8 us
    pallas_call x1, Pallas kernels, migrate(): pl.pallas_call(migrate_kernel, out_shape=jax.ShapeDtypeStruct((12, 1024),...  19.1 us
    pallas_call x1, Pallas kernels, exchange(): pl.pallas_call(exchange_kernel, out_shape=(pltpu.VMEM((3, 4 * HB, 128), F...  13.9 us

profile of v7, /device:TPU:1, one launch (start us, length us, event | category | flops | bytes accessed | tf_op | source)
XLA Modules:
  0.0 59.0 jit_solution(10654400711080756397)
XLA Ops:
  0.6 13.9 %shard_map.86 = (f32[3,256,128]{2,1,0:T(8,128)S(1)}, bf16[513,48,128]{2,1,0:T(8,128)(2,1)S(1)}, bf16[256,48,128]{2,1,0:T(8,128)(2,1)S(1)}, bf16[513,32,128]{2,1,...) custom-call(s32[4,64]{1,0:T(4,128)} %bitcast.13, s32[1,4]{1,0:T(1,128)} %counts.1, ...), custom_call_target="tpu_custom_call" | custom-call | tf_op jit(solution)/shard_map/pallas_call | solution.py:232
  14.5 24.8 %shard_map.87 = (f32[12,256,128]{2,1,0:T(8,128)}, f32[256,16,128]{2,1,0:T(8,128)S(1)}) custom-call(s32[4,256]{1,0:T(4,128)} %bitcast.11, s32[4,256]{1,0:T(4,128)} %bitcast.12, f32[12,256,128]{2,1,0:T(8,128)S(1)} %get-tuple-element.10.st, f32[3,256,128]{2,1,0:T(8,128)S(1)} %get-tuple-element.11.halo_x, bf16[513,48,128]{2,1,0:T(8,128)(2,1)S(1)} %get-tuple-element.12.feat, ...), custom_call_target="tpu_custom_call" | custom-call | tf_op jit(solution)/shard_map/pallas_call | solution.py:396
  39.3 19.1 %shard_map.88 = f32[12,1024]{1,0:T(8,128)S(1)} custom-call(s32[16,64]{1,0:T(8,128)} %bitcast.10, s32[1,64]{1,0:T(1,128)} %counts_s.1, f32[256,16,128]{2,1,0:T(8,128)S(1)} %get-tuple-element.17.upd), custom_call_target="tpu_custom_call" | custom-call | tf_op jit(solution)/shard_map/pallas_call | solution.py:472
  58.3 0.6 %copy.10 = f32[12,1024]{1,0:T(8,128)} copy(f32[12,1024]{1,0:T(8,128)S(1)} %shard_map.88) | data formatting | bytes 98304

commit v8 on v6

--- a/solution.py
+++ b/solution.py
@@ -13,7 +13,7 @@
 NC = 512
 FR = 48
 CR = 32
-U = 32
+U = 64
 RB = 4
 LOADS = 4
 REACH = 2.0
@@ -435,7 +435,9 @@
 
     lane = lax.broadcasted_iota(jnp.int32, (16, 128), 1)
 
-    def gather(g, carry):
+    def gather(k, carry):
+        g = lax.rem(place + k, 8)
+
         def to(z):
             return (g // 2) * 16 + 2 * z + g % 2
 
@@ -451,8 +453,7 @@
             message[g, :, h, :] = swap_groups(acc[8 * h : 8 * h + 8])
         return carry
 
-    lax.fori_loop(0, 8, gather, 0)
-    first[place] = message[place]
+    lax.fori_loop(1, 8, gather, 0)
     pl.semaphore_wait(barrier, 14)
 
     def hop_one(k):
@@ -480,6 +481,8 @@
     one, two = [hop_one(k) for k in range(1, 8)], [hop_two(k) for k in range(1, 8)]
     for copy in one:
         copy.start()
+    lax.fori_loop(0, 1, gather, 0)
+    first[place] = message[place]
     for copy in one:
         copy.wait_recv()
     for copy in two:

time: 59.9 us -> 59 us (0.985)
  Pallas kernels: 58.4 us -> 57.5 us
where the time goes in v8:
time: 59 us; the launch traced here: 58.8 us
  Pallas kernels  57.5 us (97%)
  between operations  0.65 us (1%)
  local copies, waits for them, and re-layouts  0.63 us (1%)
    pallas_call x1, Pallas kernels, local_step(): pl.pallas_call(local_kernel, out_shape=(pltpu.HBM((12, NB, 128), F32), pl...  24.8 us
    pallas_call x1, Pallas kernels, migrate(): pl.pallas_call(migrate_kernel, out_shape=jax.ShapeDtypeStruct((12, 1024),...  18.8 us
    pallas_call x1, Pallas kernels, exchange(): pl.pallas_call(exchange_kernel, out_shape=(pltpu.VMEM((3, 4 * HB, 128), F...  13.9 us

profile of v8, /device:TPU:1, one launch (start us, length us, event | category | flops | bytes accessed | tf_op | source)
XLA Modules:
  0.0 58.8 jit_solution(16065381029542975922)
XLA Ops:
  0.6 13.9 %shard_map.86 = (f32[3,256,128]{2,1,0:T(8,128)S(1)}, bf16[513,48,128]{2,1,0:T(8,128)(2,1)S(1)}, bf16[256,48,128]{2,1,0:T(8,128)(2,1)S(1)}, bf16[513,32,128]{2,1,...) custom-call(s32[4,64]{1,0:T(4,128)} %bitcast.13, s32[1,4]{1,0:T(1,128)} %counts.1, ...), custom_call_target="tpu_custom_call" | custom-call | tf_op jit(solution)/shard_map/pallas_call | solution.py:232
  14.5 24.8 %shard_map.87 = (f32[12,256,128]{2,1,0:T(8,128)}, f32[256,16,128]{2,1,0:T(8,128)S(1)}) custom-call(s32[4,256]{1,0:T(4,128)} %bitcast.11, s32[4,256]{1,0:T(4,128)} %bitcast.12, f32[12,256,128]{2,1,0:T(8,128)S(1)} %get-tuple-element.10.st, f32[3,256,128]{2,1,0:T(8,128)S(1)} %get-tuple-element.11.halo_x, bf16[513,48,128]{2,1,0:T(8,128)(2,1)S(1)} %get-tuple-element.12.feat, ...), custom_call_target="tpu_custom_call" | custom-call | tf_op jit(solution)/shard_map/pallas_call | solution.py:396
  39.3 18.8 %shard_map.88 = f32[12,1024]{1,0:T(8,128)S(1)} custom-call(s32[16,64]{1,0:T(8,128)} %bitcast.10, s32[1,64]{1,0:T(1,128)} %counts_s.1, f32[256,16,128]{2,1,0:T(8,128)S(1)} %get-tuple-element.17.upd), custom_call_target="tpu_custom_call" | custom-call | tf_op jit(solution)/shard_map/pallas_call | solution.py:504
  58.2 0.6 %copy.10 = f32[12,1024]{1,0:T(8,128)} copy(f32[12,1024]{1,0:T(8,128)S(1)} %shard_map.88) | data formatting | bytes 98304
